TPU v7x, 32 devices: a whole 2x2x4 slice. The times are simulated.
32 devices in a mesh: row: 8 (over y, x, core), col: 4 (over z).
Axes of the slice: x: 2, y: 2, z: 4, core: 2. Of those that a mesh axis runs over, the one named last changes fastest.
Arguments:
- density_blocks: float32 [96, 6, 256, 256], P(('row', 'col')), may hold values from -5 to 5
- density_live: int32 [96, 6], P(('row', 'col')), may hold values 0 or 1
- tangent_blocks: float32 [96, 6, 256, 256], P(('row', 'col')), may hold values from -1.5 to 1.5
- tangent_live: int32 [96, 6], P(('row', 'col')), may hold values 0 or 1
- block_offsets: int32 [96, 6], P(('row', 'col')), may hold values from -3 to 3, as said below
Outputs:
- tangent_next: float32 [96, 6, 256, 256], P(('row', 'col'))
- mean_trace: float32 [], replicated
Inputs may be any that keep to these rules, and one draw needn't show every extreme that they name: `block_offsets`: within each block row the 6 offsets are distinct and ascending.
All inputs are finite; a program needn't handle non-finite values. No bound on the sum of `density_live` or of `tangent_live` on one device may be relied on, other than what follows from the above.
Results may differ from a plain program's by a relative error of at most 0.0003.
Values sent between devices are 32-bit elements; how exact they have to be, the bound alone decides.
No kernel may reach another device: no remote copies, remote signals or barrier semaphores. Data moves between devices by JAX's collectives and lax.ppermute only.
A program may use at most 384 MiB of HBM per device.

v0:
```python
import jax
import jax.numpy as jnp
from jax import lax
from jax.sharding import PartitionSpec as P

HALF = 3


def extended_2(block, sides, width):
    for axis, dim in sides:
        count = lax.axis_size(axis)
        forward = [(i, i + 1) for i in range(count - 1)]
        forward.append((count - 1, 0))
        backward = [(target, source) for source, target in forward]
        low = lax.ppermute(
            lax.slice_in_dim(block, block.shape[dim] - width, None, axis=dim), axis, forward
        )
        high = lax.ppermute(lax.slice_in_dim(block, 0, width, axis=dim), axis, backward)
        block = jnp.concatenate([low, block, high], axis=dim)
    return block


def band_layout(values, live, offsets):
    width = 2 * HALF + 1
    places = jnp.arange(width, dtype=jnp.int32) - HALF
    select = ((offsets[:, :, None] == places[None, None, :]) & (live[:, :, None] == 1)).astype(
        values.dtype
    )
    return jnp.einsum("rsp,rsab->rpab", select, values, precision=lax.Precision.HIGHEST)


def band_product(stacked, count):
    width = 2 * HALF + 1
    result = jnp.zeros((count, width, stacked.shape[-2], stacked.shape[-1]), stacked.dtype)
    for shift_value in range(-HALF, HALF + 1):
        low_place = max(0, shift_value)
        high_place = min(2 * HALF, shift_value + 2 * HALF)
        left_blocks = stacked[HALF : HALF + count, :, shift_value + HALF]
        right_blocks = stacked[
            HALF + shift_value : HALF + shift_value + count,
            ::-1,
            low_place - shift_value : high_place - shift_value + 1,
        ]
        partial_sum = jnp.einsum(
            "rkab,rknbc->rnac", left_blocks, right_blocks, precision=lax.Precision.HIGHEST
        )
        result = result.at[:, low_place : high_place + 1].add(partial_sum)
    return result


def body(density_blocks, density_live, tangent_blocks, tangent_live, block_offsets):
    count = density_blocks.shape[0]
    own_band = jnp.stack(
        [
            band_layout(density_blocks, density_live, block_offsets),
            band_layout(tangent_blocks, tangent_live, block_offsets),
        ],
        axis=1,
    )
    extended = extended_2(own_band, ((("row", "col"), 0),), HALF)
    product = band_product(extended, count)
    chosen = jnp.take_along_axis(product, (block_offsets + HALF)[:, :, None, None], axis=1)
    weights = tangent_live.astype(jnp.float32)
    combined = 1.5 * weights[:, :, None, None] * tangent_blocks - 0.5 * chosen
    local_trace = jnp.sum(jnp.trace(product[:, HALF], axis1=1, axis2=2))
    total = count * lax.axis_size("row") * lax.axis_size("col")
    mean_trace = lax.psum(local_trace, ("row", "col")) / total
    return (combined, mean_trace)


def solution(mesh):
    return jax.shard_map(
        body,
        mesh=mesh,
        in_specs=(
            P(("row", "col"), None, None, None),
            P(("row", "col"), None),
            P(("row", "col"), None, None, None),
            P(("row", "col"), None),
            P(("row", "col"), None),
        ),
        out_specs=(P(("row", "col"), None, None, None), P()),
        check_vma=False,
    )
```

profile of v0, /device:TPU:0, one launch (start us, length us, event | category | flops | bytes accessed | tf_op | source)
XLA Modules:
  0.0 860.7 jit_solution(8349501000675173980)
XLA Ops:
  0.6 0.7 broadcast_compare_fusion.1
  1.3 0.7 broadcast_compare_fusion
  2.0 8.9 %fusion.19 = f32[3,1,7,256,256]{4,2,3,0,1:T(8,128)S(1)} fusion(f32[3,6,256,256]{3,2,1,0:T(8,128)} %param.23, s32[3,6]{1,0:T(4,128)} %param.25, s32[7]{0:T(128)S(1)} %iota_add_fusion, pred[3,6]{1,0:T(4,128)(4,1)S(1)} %broadcast_compare_fusion), kind=kOutput, calls=%fused_computation.42 | convolution fusion | flops 99090688 | bytes 10223734 | tf_op jit(solution)/shard_map/rsp,rsab->rpab/dot_general | solution.py:29
  10.9 0.0 copy-done.1
  10.9 0.0 copy-done.6
  10.9 0.0 copy-start
  11.0 7.2 fusion.16
  18.2 0.0 copy-done
  18.2 8.6 %pad_maximum_fusion = f32[3,2,7,256,256]{4,2,3,0,1:T(8,128)} fusion(f32[3,1,7,256,256]{4,2,3,0,1:T(8,128)S(1)} %fusion.19, f32[3,1,7,256,256]{4,2,3,0,1:T(8,128)} %fusion.16), kind=kLoop, calls=%fused_computation.8 | loop fusion | flops 2752512 | bytes 22020096 | tf_op jit(solution)/shard_map/stack | solution.py:53
  26.8 12.2 %copy.43 = f32[3,2,7,256,256]{4,3,2,1,0:T(8,128)} copy(f32[3,2,7,256,256]{4,2,3,0,1:T(8,128)} %pad_maximum_fusion) | data formatting | bytes 22020096 | tf_op jit(solution)/shard_map/stack | solution.py:53
  39.0 6.4 collective-permute-start.1
  45.4 0.4 collective-permute-start
  45.8 10.6 %rev.24 = f32[3,2,7,256,256]{4,2,3,0,1:T(8,128)} reverse(f32[3,2,7,256,256]{4,2,3,0,1:T(8,128)} %pad_maximum_fusion), dimensions={1} | reverse | bytes 22020096 | tf_op jit(solution)/shard_map/rev | solution.py:39
  56.5 0.7 iota_compare_fusion
  57.1 0.5 compare_and_fusion.2
  57.6 0.0 copy-done.8
  57.6 0.6 convert_multiply_fusion
  58.2 0.5 bitcast_or_fusion
  58.8 44.8 %fusion.38 = (f32[3,2,1,256,256]{4,2,3,0,1:T(1,128)S(1)}, f32[3,2,1,256,256]{4,2,3,0,1:T(1,128)}, f32[3,2,1,256,256]{4,2,3,0,1:T(1,128)}, f32[3,2,1,256,256]{4,2...) fusion(f32[3,1,7,256,256]{4,2,3,0,1:T(8,128)} %fusion.16, ...), kind=kLoop, calls=%fused_computation.50 | loop fusion | flops 2752512 | bytes 22020096 | tf_op jit(solution)/shard_map/stack | solution.py:53
  103.6 179.2 %collective-permute-done.1 = f32[3,2,7,256,256]{4,3,2,1,0:T(8,128)} collective-permute-done((f32[3,2,7,256,256]{4,3,2,1,0:T(8,128)}, f32[3,2,7,256,256]{4,3,2,1,0:T(8,128)}, u32[]{:S(2)}, u32[]{:S(2)}) %collective-permute-start.1) | collective-permute-done | bytes 11010080 | tf_op jit(solution)/shard_map/ppermute | solution.py:18
  282.8 15.1 %copy.54 = f32[3,2,7,256,256]{4,2,3,0,1:T(8,128)} copy(f32[3,2,7,256,256]{4,3,2,1,0:T(8,128)} %collective-permute-done.1) | data formatting | bytes 22020096 | tf_op jit(solution)/shard_map/ppermute | solution.py:18
  297.9 219.9 %collective-permute-done = f32[3,2,7,256,256]{4,3,2,1,0:T(8,128)} collective-permute-done((f32[3,2,7,256,256]{4,3,2,1,0:T(8,128)}, f32[3,2,7,256,256]{4,3,2,1,0:T(8,128)}, u32[]{:S(2)}, u32[]{:S(2)}) %collective-permute-start) | collective-permute-done | bytes 11010080 | tf_op jit(solution)/shard_map/ppermute | solution.py:15
  517.9 15.2 %copy.46 = f32[3,2,7,256,256]{4,2,3,0,1:T(8,128)} copy(f32[3,2,7,256,256]{4,3,2,1,0:T(8,128)} %collective-permute-done) | data formatting | bytes 22020096 | tf_op jit(solution)/shard_map/ppermute | solution.py:15
  533.0 0.0 slice-done
  533.0 0.0 slice-done.1
  533.0 29.2 %pad_maximum_fusion.1 = (f32[6,2,7,256,256]{4,2,3,0,1:T(8,128)}, f32[6,2,7,256,256]{4,2,3,0,1:T(8,128)}) fusion(f32[3,2,7,256,256]{4,2,3,0,1:T(8,128)} %copy.54, f32[3,1,7,256,256]{4,2,3,0,1:T(8,128)S(1)} %bitcast.121, f32[3,1,7,256,256]{4,2,3,0,1:T(8,128)} %fusion.16, f32[3,2,7,256,256]{4,2,3,0,1:T(8,128)} %copy.46), kind=kLoop, calls=%fused_computation.17 | loop fusion | flops 22020096 | bytes 77070336 | tf_op jit(solution)/shard_map/concatenate | solution.py:19
  562.2 10.7 %slice.282 = f32[3,2,5,256,256]{4,2,3,0,1:T(8,128)} slice(f32[6,2,7,256,256]{4,2,3,0,1:T(8,128)} %get-tuple-element.101), slice={[2:5], [0:2], [0:5], [0:256], [0:256]} | slice | bytes 15728640 | tf_op jit(solution)/shard_map/slice | solution.py:39
  572.9 10.7 %slice.278 = f32[3,2,6,256,256]{4,2,3,0,1:T(8,128)} slice(f32[6,2,7,256,256]{4,2,3,0,1:T(8,128)} %get-tuple-element.101), slice={[1:4], [0:2], [0:6], [0:256], [0:256]} | slice | bytes 18874368 | tf_op jit(solution)/shard_map/slice | solution.py:39
  583.6 10.7 %slice.272 = f32[3,2,6,256,256]{4,2,3,0,1:T(8,128)} slice(f32[6,2,7,256,256]{4,2,3,0,1:T(8,128)} %get-tuple-element.102), slice={[2:5], [0:2], [1:7], [0:256], [0:256]} | slice | bytes 18874368 | tf_op jit(solution)/shard_map/slice | solution.py:39
  594.3 10.5 %slice.268 = f32[3,2,5,256,256]{4,2,3,0,1:T(8,128)} slice(f32[6,2,7,256,256]{4,2,3,0,1:T(8,128)} %get-tuple-element.102), slice={[1:4], [0:2], [2:7], [0:256], [0:256]} | slice | bytes 15728640 | tf_op jit(solution)/shard_map/slice | solution.py:39
  604.9 6.0 slice.286
  610.9 6.0 rev.27
  616.9 6.0 slice.265
  623.0 6.0 rev.21
  629.0 10.7 %rev.25 = f32[3,2,6,256,256]{4,2,3,0,1:T(8,128)} reverse(f32[3,2,6,256,256]{4,2,3,0,1:T(8,128)} %slice.278), dimensions={1} | reverse | bytes 18874368 | tf_op jit(solution)/shard_map/rev | solution.py:39
  639.7 10.7 %rev.26 = f32[3,2,5,256,256]{4,2,3,0,1:T(8,128)} reverse(f32[3,2,5,256,256]{4,2,3,0,1:T(8,128)} %slice.282), dimensions={1} | reverse | bytes 15728640 | tf_op jit(solution)/shard_map/rev | solution.py:39
  650.4 10.7 %rev.22 = f32[3,2,5,256,256]{4,2,3,0,1:T(8,128)} reverse(f32[3,2,5,256,256]{4,2,3,0,1:T(8,128)} %slice.268), dimensions={1} | reverse | bytes 15728640 | tf_op jit(solution)/shard_map/rev | solution.py:39
  661.0 10.7 %rev.23 = f32[3,2,6,256,256]{4,2,3,0,1:T(8,128)} reverse(f32[3,2,6,256,256]{4,2,3,0,1:T(8,128)} %slice.272), dimensions={1} | reverse | bytes 18874368 | tf_op jit(solution)/shard_map/rev | solution.py:39
  671.7 12.7 %convolution_bitcast_fusion = f32[3,4,256,256]{2,3,1,0:T(8,128)S(1)} fusion(f32[3,2,4,256,256]{4,3,2,1,0:T(8,128)} %rev.21, f32[3,2,1,256,256]{4,2,3,0,1:T(1,128)} %get-tuple-element.95), kind=kOutput, calls=%fused_computation.43 | convolution fusion | flops 4831838208 | bytes 11010048 | tf_op jit(solution)/shard_map/rkab,rknbc->rnac/dot_general | solution.py:44
  684.4 0.0 copy-start.3
  684.4 0.5 scatter-add.20
  684.9 0.9 copy-done.3
  685.8 17.3 %fusion.15 = f32[3,7,256,256]{2,3,1,0:T(8,128)S(1)} fusion(f32[3,7,256,256]{2,3,1,0:T(8,128)S(1)} %scatter-add.20, f32[3,2,5,256,256]{4,2,3,0,1:T(8,128)} %rev.22, f32[3,2,1,256,256]{4,2,3,0,1:T(1,128)S(1)} %copy-done.3), kind=kOutput, calls=%fused_computation.39 | convolution fusion | flops 6040780800 | bytes 17301504 | tf_op jit(solution)/shard_map/rkab,rknbc->rnac/dot_general | solution.py:44
  703.2 0.0 copy-done.2
  703.2 0.0 slice-start.4
  703.2 20.7 %fusion.14 = f32[3,7,256,256]{2,3,1,0:T(8,128)S(1)} fusion(f32[3,7,256,256]{2,3,1,0:T(8,128)S(1)} %fusion.15, f32[3,2,6,256,256]{4,2,3,0,1:T(8,128)} %rev.23, f32[3,2,1,256,256]{4,2,3,0,1:T(1,128)S(1)} %copy-done.2), kind=kOutput, calls=%fused_computation.35 | convolution fusion | flops 7248936960 | bytes 20447232 | tf_op jit(solution)/shard_map/rkab,rknbc->rnac/dot_general | solution.py:44
  723.9 0.0 slice-done.2
  723.9 0.0 slice-done.3
  723.9 0.0 slice-done.4
  724.0 0.0 slice-start.5
  724.0 21.9 %bitcast_add_fusion = f32[3,7,256,256]{2,3,1,0:T(8,128)} fusion(f32[3,7,256,256]{2,3,1,0:T(8,128)S(1)} %fusion.14, f32[3,2,7,256,256]{4,2,3,0,1:T(8,128)S(1)} %bitcast.123, f32[3,2,1,256,256]{4,2,3,0,1:T(1,128)} %get-tuple-element.98), kind=kOutput, calls=%fused_computation.32 | convolution fusion | flops 8457093120 | bytes 23592960 | tf_op jit(solution)/shard_map/rkab,rknbc->rnac/dot_general | solution.py:44
  745.9 21.6 %constant_dynamic-update-slice_fusion.2 = (f32[3,7,256,256]{2,3,1,0:T(8,128)}, f32[3,6,256,256]{2,3,1,0:T(8,128)S(1)}) fusion(f32[3,7,256,256]{2,3,1,0:T(8,128)} %bitcast_add_fusion, f32[3,2,1,256,256]{4,2,3,0,1:T(1,128)S(1)} %get-tuple-element.99, f32[3,2,6,256,256]{4,2,3,0,1:T(8,128)} %rev.25), kind=kOutput, calls=%fused_computation.85 | convolution fusion | flops 7248936960 | bytes 28311552 | tf_op jit(solution)/shard_map/rkab,rknbc->rnac/dot_general | solution.py:44
  767.5 0.0 copy-done.4
  767.5 18.7 %constant_dynamic-update-slice_fusion.1 = (f32[3,7,256,256]{2,3,1,0:T(8,128)}, f32[3,5,256,256]{2,3,1,0:T(8,128)S(1)}) fusion(f32[3,7,256,256]{2,3,1,0:T(8,128)} %get-tuple-element.103, f32[3,2,1,256,256]{4,2,3,0,1:T(1,128)S(1)} %copy-done.4, f32[3,2,5,256,256]{4,2,3,0,1:T(8,128)} %rev.26, f32[3,6,256,256]{2,3,1,0:T(8,128)S(1)} %get-tuple-element.104), kind=kOutput, calls=%fused_computation.84 | convolution fusion | flops 6040780800 | bytes 25952256 | tf_op jit(solution)/shard_map/rkab,rknbc->rnac/dot_general | solution.py:44
  786.2 0.0 slice-done.5
  786.2 0.0 slice-done.6
  786.3 12.1 %constant_dynamic-update-slice_fusion = (f32[3,7,256,256]{2,3,1,0:T(8,128)}, f32[3,4,256,256]{2,3,1,0:T(8,128)S(1)}) fusion(f32[3,7,256,256]{2,3,1,0:T(8,128)} %get-tuple-element.105, f32[3,2,4,256,256]{4,3,2,1,0:T(8,128)S(1)} %bitcast.125, f32[3,2,1,256,256]{4,2,3,0,1:T(1,128)S(1)} %get-tuple-element.94, f32[3,5,256,256]{2,3,1,0:T(8,128)S(1)} %get-tuple-element.106), kind=kOutput, calls=%fused_computation.83 | convolution fusion | flops 4832624640 | bytes 17301504 | tf_op jit(solution)/shard_map/rkab,rknbc->rnac/dot_general | solution.py:44
  798.3 0.0 copy-done.5
  798.3 0.8 fusion.54
  799.1 0.1 reshape.275
  799.2 40.5 %psum.7 = f32[]{:T(128)} all-reduce(f32[]{:T(128)} %fusion.54), channel_id=1, replica_groups=mesh['row'=8,'col'=4] {'row','col'}, use_global_device_ids=true, to_apply=%region_1.0 | all-reduce | flops 1 | bytes 8 | tf_op jit(solution)/shard_map/psum | solution.py:67
  839.8 5.8 gather_fusion
  845.6 6.1 copy.61
  852.4 7.0 multiply_subtract_fusion
  (21 shorter events, 0.0 us)
Async XLA Ops:
  2.0 8.9 %copy-start.1 = (f32[3,6,256,256]{3,2,1,0:T(8,128)S(1)}, f32[3,6,256,256]{3,2,1,0:T(8,128)}, u32[]{:S(2)}) copy-start(f32[3,6,256,256]{3,2,1,0:T(8,128)} %param.21) | copy-start | bytes 14155780
  2.0 8.9 %copy-start.6 = (s32[3,6]{1,0:T(4,128)S(1)}, s32[3,6]{1,0:T(4,128)}, u32[]{:S(2)}) copy-start(s32[3,6]{1,0:T(4,128)} %param.25) | copy-start | bytes 220
  10.9 7.2 copy-start
  39.0 18.6 %copy-start.8 = (s32[3,6]{1,0:T(4,128)S(1)}, s32[3,6]{1,0:T(4,128)}, u32[]{:S(2)}) copy-start(s32[3,6]{1,0:T(4,128)} %param.24) | copy-start | bytes 220
  39.0 243.8 %collective-permute-start.1 = (f32[3,2,7,256,256]{4,3,2,1,0:T(8,128)}, f32[3,2,7,256,256]{4,3,2,1,0:T(8,128)}, u32[]{:S(2)}, u32[]{:S(2)}) collective-permute-start(f32[3,2,7,256,256]{4,3,2,1,0:T(8,128)} %copy.43), channel_id=1, source_target_pairs={{1,0},{2,1},{3,2},{4,3},{5,4},{6,5},{7,6},{8,7},{9,8},{10,9},{11,1... | collective-permute-start | bytes 33030152 | tf_op jit(solution)/shard_map/ppermute | solution.py:18
  45.4 472.5 %collective-permute-start = (f32[3,2,7,256,256]{4,3,2,1,0:T(8,128)}, f32[3,2,7,256,256]{4,3,2,1,0:T(8,128)}, u32[]{:S(2)}, u32[]{:S(2)}) collective-permute-start(f32[3,2,7,256,256]{4,3,2,1,0:T(8,128)} %copy.43), channel_id=1, source_target_pairs={{0,1},{1,2},{2,3},{3,4},{4,5},{5,6},{6,7},{7,8},{8,9},{9,10},{10,1... | collective-permute-start | bytes 33030152 | tf_op jit(solution)/shard_map/ppermute | solution.py:15
  282.8 250.2 %slice-start = ((s8[6291456]{0:T(1024)(128)(4,1)}), s8[4194304]{0:T(1024)(128)(4,1)S(1)}, s32[]{:S(2)}) async-start(s8[6291456]{0:T(1024)(128)(4,1)} %bitcast.120), calls=%async_computation | async-start | bytes 8388608
  297.9 235.1 %slice-start.1 = ((s8[6291456]{0:T(1024)(128)(4,1)}), s8[2097152]{0:T(1024)(128)(4,1)S(1)}, s32[]{:S(2)}) async-start(s8[6291456]{0:T(1024)(128)(4,1)} %bitcast.120), calls=%async_computation.1 | async-start | bytes 4194304
  684.4 1.4 copy-start.3
  685.8 17.4 %copy-start.2 = (f32[3,2,1,256,256]{4,2,3,0,1:T(1,128)S(1)}, f32[3,2,1,256,256]{4,2,3,0,1:T(1,128)}, u32[]{:S(2)}) copy-start(f32[3,2,1,256,256]{4,2,3,0,1:T(1,128)} %get-tuple-element.97) | copy-start | bytes 4718596
  685.8 38.1 %slice-start.2 = ((s8[12582912]{0:T(1024)(128)(4,1)}), s8[4194304]{0:T(1024)(128)(4,1)S(1)}, s32[]{:S(2)}) async-start(s8[12582912]{0:T(1024)(128)(4,1)} %bitcast.122), calls=%async_computation.2 | async-start | bytes 8388608
  685.8 38.1 %slice-start.3 = ((s8[12582912]{0:T(1024)(128)(4,1)}), s8[4194304]{0:T(1024)(128)(4,1)S(1)}, s32[]{:S(2)}) async-start(s8[12582912]{0:T(1024)(128)(4,1)} %bitcast.122), calls=%async_computation.3 | async-start | bytes 8388608
  703.2 20.8 %slice-start.4 = ((s8[12582912]{0:T(1024)(128)(4,1)}), s8[4194304]{0:T(1024)(128)(4,1)S(1)}, s32[]{:S(2)}) async-start(s8[12582912]{0:T(1024)(128)(4,1)} %bitcast.122), calls=%async_computation.4 | async-start | bytes 8388608
  724.0 62.3 %slice-start.5 = ((s8[6291456]{0:T(1024)(128)(4,1)}), s8[2097152]{0:T(1024)(128)(4,1)S(1)}, s32[]{:S(2)}) async-start(s8[6291456]{0:T(1024)(128)(4,1)} %bitcast.124), calls=%async_computation.5 | async-start | bytes 4194304
  745.9 21.6 %copy-start.4 = (f32[3,2,1,256,256]{4,2,3,0,1:T(1,128)S(1)}, f32[3,2,1,256,256]{4,2,3,0,1:T(1,128)}, u32[]{:S(2)}) copy-start(f32[3,2,1,256,256]{4,2,3,0,1:T(1,128)} %get-tuple-element.100) | copy-start | bytes 4718596
  745.9 40.3 %slice-start.6 = ((s8[6291456]{0:T(1024)(128)(4,1)}), s8[4194304]{0:T(1024)(128)(4,1)S(1)}, s32[]{:S(2)}) async-start(s8[6291456]{0:T(1024)(128)(4,1)} %bitcast.124), calls=%async_computation.6 | async-start | bytes 8388608
  786.2 12.1 %copy-start.5 = (pred[256,256]{0,1:T(8,128)(4,1)S(1)}, pred[256,256]{0,1:T(8,128)(4,1)}, u32[]{:S(2)}) copy-start(pred[256,256]{0,1:T(8,128)(4,1)} %iota_compare_fusion) | copy-start | bytes 196612
  786.2 12.9 %copy-start.9 = (s32[3,6,1]{1,0,2:T(4,128)S(1)}, s32[3,6,1]{1,0,2:T(4,128)}, u32[]{:S(2)}) copy-start(s32[3,6,1]{1,0,2:T(4,128)} %bitcast_or_fusion) | copy-start | bytes 220
  845.6 6.7 copy-start.7
  845.6 6.7 copy-start.10
where the time goes:
time: 870 us; the launch traced here: 861 us
  waiting for transfers between devices  399 us (46%)
  local copies, waits for them, and re-layouts  176 us (20%)
  matrix products  141 us (16%)
  other arithmetic  94.1 us (11%)
  blocking collectives  40.5 us (5%)
    ppermute x1, waiting for transfers between devices, extended_2(): lax.ppermute(lax.slice_in_dim(block, block.shape[dim] - width, None, axis...  220 us
    ppermute x1, waiting for transfers between devices, extended_2(): lax.ppermute(lax.slice_in_dim(block, 0, width, axis=dim), axis, backward)  179 us
    dot_general x7, matrix products, band_product(): jnp.einsum('rkab,rknbc->rnac', left_blocks, right_blocks, precision=lax.P...  125 us
    rev x7, local copies, waits for them, and re-layouts, band_product(): stacked[HALF + shift_value:HALF + shift_value + count, ::-1, low_place -...  65.4 us
    slice x6, local copies, waits for them, and re-layouts, band_product(): stacked[HALF + shift_value:HALF + shift_value + count, ::-1, low_place -...  54.8 us
    another operation x2, other arithmetic, body(): jnp.stack([band_layout(density_blocks, density_live, block_offsets), band...  53.5 us
    psum x1, blocking collectives, body(): mean_trace = lax.psum(local_trace, ('row', 'col')) / total  40.5 us
    concatenate x1, other arithmetic, extended_2(): block = jnp.concatenate([low, block, high], axis=dim)  29.2 us
  transfers between devices with their start and end apart: 2, of which 2 were waited for; matrix products, arithmetic and copies ran while one was open for 8% of the time, Pallas kernels for 0%

commit v1 on v0

v1 whole, which is shorter than its diff:
```python
import functools

import jax
import jax.numpy as jnp
from jax import lax
from jax.experimental import pallas as pl
from jax.experimental.pallas import tpu as pltpu
from jax.sharding import PartitionSpec as P

HALF = 3
WIDTH = 2 * HALF + 1
WIN = 2 * HALF
AXES = ("row", "col")
VMEM_LIMIT = 58 * 1024 * 1024
F32 = jnp.float32
BF16 = jnp.bfloat16
I32 = jnp.int32


def need_cells(side):
    base = 0 if side == 0 else HALF
    return [
        (t, k, j)
        for t in range(2)
        for k in range(HALF)
        for j in range(WIN)
        if abs(j - (base + k)) <= HALF
    ]


def cell(t, k, j):
    return (t * HALF + k) * WIN + j


CELLS = 2 * HALF * WIN
COUNT_ROW = 2 * CELLS
PLAN_ROWS = 2 * CELLS + 8


def plan_kernel(slots, me_ref, meta_ref, out_ref, table):
    n = meta_ref.shape[-1]
    fields = 3 * slots

    def row(i, f):
        source, r = (0, i) if i < HALF else (1, i - HALF)
        at = r * fields + f
        return meta_ref[source, at : at + 1, :]

    one = jnp.ones((1, n), I32)
    zero = jnp.zeros((1, n), I32)
    live = [{}, {}]
    stored = {}
    for i in range(WIN):
        offs = [row(i, 2 * slots + s) for s in range(slots)]
        flags = [[jnp.where(row(i, t * slots + s) == 1, one, zero) for s in range(slots)] for t in range(2)]
        for j in range(WIN):
            d = j - i
            if abs(d) > HALF:
                continue
            here = [jnp.where(o == d, one, zero) for o in offs]
            stored[i, j] = one if d == 0 else functools.reduce(jnp.bitwise_or, here)
            for t in range(2):
                live[t][i, j] = functools.reduce(jnp.bitwise_or, [h & f for h, f in zip(here, flags[t])])

    table[...] = jnp.full(table.shape, -1, I32)
    most = zero
    for side in range(2):
        base, other = (0, HALF) if side == 0 else (HALF, 0)
        count = zero
        for t, k, j in need_cells(side):
            kk = base + k
            users = [
                live[1 - t][i, kk] & stored[i, j]
                for i in range(other, other + HALF)
                if abs(i - kk) <= HALF and abs(j - i) <= HALF
            ]
            need = functools.reduce(jnp.bitwise_or, users) & live[t][kk, j]
            at = side * CELLS + cell(t, k, j)
            table[at : at + 1, :] = jnp.where(need == 1, count, -one)
            count = count + need
        table[COUNT_ROW + side : COUNT_ROW + side + 1, :] = count
        most = jnp.maximum(most, count)
    top = jnp.max(most.astype(F32), axis=1, keepdims=True).astype(I32)
    table[COUNT_ROW + 2 : COUNT_ROW + 3, :] = jnp.broadcast_to(top, (1, n))

    me = me_ref[0]
    whole = table[...]
    lane = lax.broadcasted_iota(I32, whole.shape, 1)
    right = lax.rem(me + 1, n)
    first = jnp.sum(jnp.where(lane == me, whole, 0), axis=1, keepdims=True)
    second = jnp.sum(jnp.where(lane == right, whole, 0), axis=1, keepdims=True)
    out_lane = lax.broadcasted_iota(I32, out_ref.shape, 1)
    out_ref[...] = jnp.where(out_lane == 0, first, second)


def make_plan(meta, me, slots):
    n, rows = meta.shape[0], meta.shape[1]
    low = jnp.roll(meta[:, rows - HALF :], 1, axis=0).reshape(n, -1).T
    high = meta[:, :HALF].reshape(n, -1).T
    return pl.pallas_call(
        functools.partial(plan_kernel, slots),
        out_shape=jax.ShapeDtypeStruct((PLAN_ROWS, 128), I32),
        in_specs=[pl.BlockSpec(memory_space=pltpu.SMEM), pl.BlockSpec(memory_space=pltpu.VMEM)],
        out_specs=pl.BlockSpec(memory_space=pltpu.VMEM),
        scratch_shapes=[pltpu.VMEM((PLAN_ROWS, n), I32)],
        name="plan",
    )(me.reshape(1), jnp.stack([low, high]))


def pack_kernel(rows, own_ref, forth_ref, back_ref, x_ref, t_ref, forth_out, back_out, sems):
    stored = x_ref.shape[0]

    def each(act):
        index = 0
        for side, at_ref, out in ((0, forth_ref, forth_out), (1, back_ref, back_out)):
            for t, k, j in need_cells(side):
                own_row = rows - HALF + k if side == 0 else k
                place = j - k + HALF if side == 0 else j - k
                at = at_ref[cell(t, k, j)]
                source = (x_ref, t_ref)[t]
                sem = sems.at[index]
                index += 1

                @pl.when(at >= 0)
                def _():
                    block = own_ref[(t * rows + own_row) * WIDTH + place] - t * stored
                    act(pltpu.make_async_copy(source.at[block], out.at[at], sem))

    each(lambda copy: copy.start())
    each(lambda copy: copy.wait())


def pack(own, forth, back, x, t, room, rows):
    smem = pl.BlockSpec(memory_space=pltpu.SMEM)
    hbm = pl.BlockSpec(memory_space=pl.ANY)
    shape = jax.ShapeDtypeStruct((room,) + x.shape[1:], F32)
    return pl.pallas_call(
        functools.partial(pack_kernel, rows),
        out_shape=(shape, shape),
        in_specs=[smem, smem, smem, hbm, hbm],
        out_specs=(hbm, hbm),
        scratch_shapes=[pltpu.SemaphoreType.DMA((2 * len(need_cells(0)),))],
        name="pack",
    )(own, forth, back, x, t)


def halves(values):
    high = values.astype(BF16)
    return high, (values - high.astype(F32)).astype(BF16)


def product(lh, ll, rh, rl):
    dot = functools.partial(jnp.dot, preferred_element_type=F32)
    return dot(lh, rh) + (dot(lh, rl) + dot(ll, rh))


def own_kernel(
    rows, slots, room,
    own_ref, left_ref, right_ref, off_ref, x_ref, t_ref,
    part_ref, high_ref, low_ref, lists_ref,
    local_ref,
):
    stored = rows * slots
    outs = stored + rows

    def split(i, carry):
        for t, source in enumerate((x_ref, t_ref)):
            high, low = halves(source[i])
            high_ref[t * stored + i] = high
            low_ref[t * stored + i] = low
        return carry

    lax.fori_loop(0, stored, split, 0)

    def of_output(q, counts):
        is_diag = q >= stored
        row = jnp.where(is_diag, q - stored, lax.div(q, slots))
        d = jnp.where(is_diag, 0, off_ref[jnp.minimum(q, stored - 1)])
        has_zero = jnp.bool_(False)
        for s in range(slots):
            has_zero = has_zero | (off_ref[row * slots + s] == 0)
        wanted = jnp.logical_not(is_diag & has_zero)
        lists_ref[2, q] = counts[1]
        local_ref[2, q] = counts[0]

        def of_term(m, counts):
            t = lax.rem(m, 2)
            e = lax.div(m, 2) - HALF
            k = row + e
            place = d - e + HALF
            ok = wanted & (place >= 0) & (place < WIDTH)
            left = own_ref[(t * rows + row) * WIDTH + e + HALF]
            ok = ok & (left >= 0)
            column = row + d
            own_side = (k >= 0) & (k < rows)
            own_at = jnp.where(ok & own_side, ((1 - t) * rows + k) * WIDTH + place, 0)
            own_block = own_ref[own_at]
            low_at = jnp.where(ok & (k < 0), ((1 - t) * HALF + k + HALF) * WIN + column + HALF, 0)
            low_block = left_ref[low_at]
            high_at = jnp.where(
                ok & (k >= rows), ((1 - t) * HALF + k - rows) * WIN + column - rows + HALF, 0
            )
            high_block = right_ref[high_at]
            far_block = jnp.where(k < 0, low_block, high_block)
            far_place = jnp.where(k < 0, low_block, high_block + room)
            near, far = counts
            local_ref[0, near] = left
            local_ref[1, near] = own_block
            near = near + jnp.where(ok & own_side & (own_block >= 0), 1, 0)
            lists_ref[0, far] = left
            lists_ref[1, far] = far_place
            far = far + jnp.where(ok & jnp.logical_not(own_side) & (far_block >= 0), 1, 0)
            return near, far

        return lax.fori_loop(0, 2 * WIDTH, of_term, counts)

    near, far = lax.fori_loop(0, outs, of_output, (jnp.int32(0), jnp.int32(0)))
    lists_ref[2, outs] = far
    local_ref[2, outs] = near

    def compute(q, carry):
        part_ref[q] = jnp.zeros(part_ref.shape[1:], F32)

        def term(m, carry):
            left = local_ref[0, m]
            right = local_ref[1, m]
            part_ref[q] += product(high_ref[left], low_ref[left], high_ref[right], low_ref[right])
            return carry

        return lax.fori_loop(local_ref[2, q], local_ref[2, q + 1], term, carry)

    lax.fori_loop(0, outs, compute, 0)


def list_length(rows, slots):
    return -(-((rows * slots + rows) * 2 * WIDTH + 1) // 128) * 128


def own_part(own, left, right, offsets, x, t, room, rows, slots):
    smem = pl.BlockSpec(memory_space=pltpu.SMEM)
    vmem = pl.BlockSpec(memory_space=pltpu.VMEM)
    stored = rows * slots
    block = x.shape[1:]
    length = list_length(rows, slots)
    return pl.pallas_call(
        functools.partial(own_kernel, rows, slots, room),
        out_shape=(
            jax.ShapeDtypeStruct((stored + rows,) + block, F32),
            jax.ShapeDtypeStruct((2 * stored,) + block, BF16),
            jax.ShapeDtypeStruct((2 * stored,) + block, BF16),
            jax.ShapeDtypeStruct((3, length), I32),
        ),
        in_specs=[smem, smem, smem, smem, vmem, vmem],
        out_specs=(vmem, vmem, vmem, smem),
        scratch_shapes=[pltpu.SMEM((3, length), I32)],
        compiler_params=pltpu.CompilerParams(vmem_limit_bytes=VMEM_LIMIT),
        cost_estimate=pl.CostEstimate(
            flops=60 * 3 * 2 * block[0] ** 3, bytes_accessed=30 * 2**20, transcendentals=0
        ),
        name="own_rows",
    )(own, left, right, offsets, x, t)


def halo_kernel(
    rows, slots, room,
    lists_ref, counts_ref, off_ref, weight_ref,
    low_ref, high_ref, own_high_ref, own_low_ref, part_ref, t_ref,
    out_ref, trace_ref,
    stage, far_high, far_low, own_high, own_low, total, tangent, stage_sems, sems,
):
    stored = rows * slots
    outs = stored + rows
    copies = [
        pltpu.make_async_copy(source, target, sems.at[i])
        for i, (source, target) in enumerate(
            ((own_high_ref, own_high), (own_low_ref, own_low), (part_ref, total), (t_ref, tangent))
        )
    ]
    for copy in copies:
        copy.start()
    depth = stage.shape[0]

    for side, source in enumerate((low_ref, high_ref)):
        count = counts_ref[side]

        def fetch(i):
            slot = lax.rem(i, depth)
            return pltpu.make_async_copy(source.at[i], stage.at[slot], stage_sems.at[slot])

        for i in range(depth - 1):

            @pl.when(i < count)
            def _():
                fetch(i).start()

        def convert(i, carry):
            @pl.when(i + depth - 1 < count)
            def _():
                fetch(i + depth - 1).start()

            fetch(i).wait()
            high, low = halves(stage[lax.rem(i, depth)])
            far_high[side * room + i] = high
            far_low[side * room + i] = low
            return carry

        lax.fori_loop(0, count, convert, 0)

    for copy in copies:
        copy.wait()

    block = total.shape[1:]
    eye = lax.broadcasted_iota(I32, block, 0) == lax.broadcasted_iota(I32, block, 1)
    trace_ref[0, 0] = jnp.float32(0)

    def compute(q, carry):
        def term(m, carry):
            left = lists_ref[0, m]
            right = lists_ref[1, m]
            total[q] += product(own_high[left], own_low[left], far_high[right], far_low[right])
            return carry

        lax.fori_loop(lists_ref[2, q], lists_ref[2, q + 1], term, 0)

        @pl.when(q < stored)
        def _():
            at = jnp.minimum(q, stored - 1)
            scale = 1.5 * weight_ref[at].astype(F32)
            out_ref[at] = scale * tangent[at] - 0.5 * total[q]

        @pl.when((q >= stored) | (off_ref[jnp.minimum(q, stored - 1)] == 0))
        def _():
            trace_ref[0, 0] += jnp.sum(jnp.where(eye, total[q], 0.0))

        return carry

    lax.fori_loop(0, outs, compute, 0)


def halo_part(lists, counts, offsets, weights, low, high, own_high, own_low, part, t, rows, slots):
    smem = pl.BlockSpec(memory_space=pltpu.SMEM)
    vmem = pl.BlockSpec(memory_space=pltpu.VMEM)
    hbm = pl.BlockSpec(memory_space=pl.ANY)
    room = low.shape[0]
    stored = rows * slots
    block = t.shape[1:]
    return pl.pallas_call(
        functools.partial(halo_kernel, rows, slots, room),
        out_shape=(
            jax.ShapeDtypeStruct((stored,) + block, F32),
            jax.ShapeDtypeStruct((1, 1), F32),
        ),
        in_specs=[smem] * 4 + [hbm] * 6,
        out_specs=(vmem, smem),
        scratch_shapes=[
            pltpu.VMEM((4,) + block, F32),
            pltpu.VMEM((2 * room,) + block, BF16),
            pltpu.VMEM((2 * room,) + block, BF16),
            pltpu.VMEM((2 * stored,) + block, BF16),
            pltpu.VMEM((2 * stored,) + block, BF16),
            pltpu.VMEM((stored + rows,) + block, F32),
            pltpu.VMEM((stored,) + block, F32),
            pltpu.SemaphoreType.DMA((4,)),
            pltpu.SemaphoreType.DMA((4,)),
        ],
        compiler_params=pltpu.CompilerParams(vmem_limit_bytes=VMEM_LIMIT),
        cost_estimate=pl.CostEstimate(
            flops=60 * 3 * 2 * block[0] ** 3, bytes_accessed=30 * 2**20, transcendentals=0
        ),
        name="halo_rows",
    )(lists, counts, offsets, weights, low, high, own_high, own_low, part, t)


def body(density_blocks, density_live, tangent_blocks, tangent_live, block_offsets):
    rows, slots = density_live.shape
    block = density_blocks.shape[2:]
    n = lax.axis_size("row") * lax.axis_size("col")
    me = lax.axis_index(AXES).astype(I32)
    x = density_blocks.reshape((rows * slots,) + block)
    t = tangent_blocks.reshape((rows * slots,) + block)
    offsets = block_offsets.reshape(-1)
    weights = tangent_live.reshape(-1)

    meta = jnp.concatenate([density_live, tangent_live, block_offsets], axis=1)
    gathered = lax.all_gather(meta, AXES, tiled=True).reshape(n, rows, 3 * slots)
    plan = make_plan(gathered, me, slots)
    left, right = plan[:, 0], plan[:, 1]
    from_low, to_low = left[:CELLS], left[CELLS : 2 * CELLS]
    to_high, from_high = right[:CELLS], right[CELLS : 2 * CELLS]
    counts = jnp.stack([left[COUNT_ROW], right[COUNT_ROW + 1]])

    index = jnp.arange(rows * slots, dtype=I32).reshape(rows, slots, 1)
    here = block_offsets[:, :, None] == jnp.arange(-HALF, HALF + 1, dtype=I32)
    own = jnp.stack(
        [
            jnp.max(jnp.where(here & (live == 1)[:, :, None], index + shift, -1), axis=1)
            for live, shift in ((density_live, 0), (tangent_live, rows * slots))
        ]
    ).reshape(-1)

    forward = [(i, (i + 1) % n) for i in range(n)]
    backward = [(b, a) for a, b in forward]

    def with_room(room, own, left, right, offsets, weights, counts, to_high, to_low, x, t):
        forth, back = pack(own, to_high, to_low, x, t, room, rows)
        low = lax.ppermute(forth, AXES, forward)
        high = lax.ppermute(back, AXES, backward)
        part, own_high, own_low, lists = own_part(own, left, right, offsets, x, t, room, rows, slots)
        return halo_part(
            lists, counts, offsets, weights, low, high, own_high, own_low, part, t, rows, slots
        )

    worst = len(need_cells(0))
    rooms = [r for r in (12, 15, 16, 17, 18, 19, 20, 21, 22, 23, 24, 26) if r < worst] + [worst]
    choice = jnp.sum((left[COUNT_ROW + 2] > jnp.array(rooms[:-1], I32)).astype(I32))
    out, trace = lax.switch(
        choice,
        [functools.partial(with_room, room) for room in rooms],
        own, from_low, from_high, offsets, weights, counts, to_high, to_low, x, t,
    )
    mean_trace = lax.psum(trace[0, 0], AXES) / (rows * n)
    return out.reshape(tangent_blocks.shape), mean_trace


def solution(mesh):
    return jax.shard_map(
        body,
        mesh=mesh,
        in_specs=(
            P(AXES, None, None, None),
            P(AXES, None),
            P(AXES, None, None, None),
            P(AXES, None),
            P(AXES, None),
        ),
        out_specs=(P(AXES, None, None, None), P()),
        check_vma=False,
    )
```

time: 870 us -> 667 us (0.77); the launches traced: 861 us -> 674 us
  Pallas kernels: 0 us -> 324 us
  waiting for transfers between devices: 399 us -> 220 us
  local copies, waits for them, and re-layouts: 176 us -> 3.77 us
  matrix products: 141 us -> 0 us
  other arithmetic: 94.1 us -> 6.28 us
  blocking collectives: 40.5 us -> 111 us
    pallas_call x0 -> x4, Pallas kernels: none -> 324 us  [the longest x1 265 us: pack(): pl.pallas_call(functools.partial(pack_kernel, rows), out_shape=(shape, sh...]
    ppermute x2, waiting for transfers between devices: 399 us -> 220 us  [the longest x1 128 us: with_room(): high = lax.ppermute(back, AXES, backward)]
    dot_general x9 -> x0, matrix products: 141 us -> none  [the longest x7 125 us: band_product(): jnp.einsum('rkab,rknbc->rnac', left_blocks, right_blocks, precision=lax.P...]
    all_gather x0 -> x1, blocking collectives: none -> 70.1 us  [body(): lax.all_gather(meta, AXES, tiled=True).reshape(n, rows, 3 * slots)]
    rev x7 -> x0, local copies, waits for them, and re-layouts: 65.4 us -> none  [band_product(): stacked[HALF + shift_value:HALF + shift_value + count, ::-1, low_place -...]
    slice x6 -> x4, local copies, waits for them, and re-layouts: 54.8 us -> 1.28 us  [the longest x1 0.66 us: body(): from_low, to_low = (left[:CELLS], left[CELLS:2 * CELLS])]
    another operation x2 -> x4, other arithmetic: 53.5 us -> 2.09 us  [the longest x1 1.37 us: body(): counts = jnp.stack([left[COUNT_ROW], right[COUNT_ROW + 1]])]
    ppermute x2 -> x0, local copies, waits for them, and re-layouts: 30.3 us -> none  [the longest x1 15.2 us: extended_2(): lax.ppermute(lax.slice_in_dim(block, block.shape[dim] - width, None, axis...]
  transfers between devices with their start and end apart: 2 -> 2, of which waited for: 2 -> 2; matrix products, arithmetic and copies ran while one was open for 8% -> 0% of each run, Pallas kernels for 0% -> 5%
where the time goes in v1:
time: 667 us; the launch traced here: 674 us
  Pallas kernels  324 us (49%)
  waiting for transfers between devices  220 us (33%)
  blocking collectives  111 us (17%)
    pallas_call x1, Pallas kernels, pack(): pl.pallas_call(functools.partial(pack_kernel, rows), out_shape=(shape, sh...  265 us
    ppermute x1, waiting for transfers between devices, with_room(): high = lax.ppermute(back, AXES, backward)  128 us
    ppermute x1, waiting for transfers between devices, with_room(): low = lax.ppermute(forth, AXES, forward)  92.4 us
    all_gather x1, blocking collectives, body(): lax.all_gather(meta, AXES, tiled=True).reshape(n, rows, 3 * slots)  70.1 us
    psum x1, blocking collectives, body(): mean_trace = lax.psum(trace[0, 0], AXES) / (rows * n)  40.7 us
    pallas_call x1, Pallas kernels, own_part(): pl.pallas_call(functools.partial(own_kernel, rows, slots, room), out_shap...  31.6 us
    pallas_call x1, Pallas kernels, halo_part(): pl.pallas_call(functools.partial(halo_kernel, rows, slots, room), out_sha...  26.5 us
  transfers between devices with their start and end apart: 2, of which 2 were waited for; matrix products, arithmetic and copies ran while one was open for 0% of the time, Pallas kernels for 5%

profile of v1, /device:TPU:0, one launch (start us, length us, event | category | flops | bytes accessed | tf_op | source)
XLA Modules:
  0.0 673.7 jit_solution(16446581086960743449)
XLA Ops:
  0.6 0.8 add_bitcast_fusion.1
  1.4 70.1 %all-gather = s32[32,3,18]{2,1,0:T(4,128)S(1)} all-gather(s32[1,3,18]{2,1,0:T(4,128)S(1)} %add_bitcast_fusion.1), channel_id=1, replica_groups=mesh['row'=8,'col'=4] {'row','col'}, dimensions={0}, use_global_device_ids=true | all-gather | bytes 7128 | tf_op jit(solution)/shard_map/all_gather | solution.py:385
  71.6 0.1 reshape.358
  71.7 0.1 copy.72
  71.8 0.1 concatenate.16
  71.9 0.1 add_bitcast_fusion
  72.0 0.1 reshape.359
  72.0 0.1 copy.73
  72.1 0.6 pad_add_fusion.meta_ref
  72.8 1.2 plan.1
  74.0 0.6 fusion.1
  74.6 1.4 pad_add_fusion.2
  76.0 0.7 broadcast_compare_fusion
  76.7 0.8 select_reduce_fusion.1
  77.5 1.9 fusion
  80.0 551.2 %conditional.1 = (f32[1,1]{1,0:T(1,128)}, f32[3,6,256,256]{3,2,1,0:T(8,128)}) conditional(s32[]{:T(128)} %clamp.3, (s32[2,3,7]{2,1,0:T(4,128)S(1)}, s32[80,128]{1,0:T(8,128)S(1)}, s32[3,6]{1,0:T(4,128)}, f32[3,6,256,256]{3,2,1,0:T(8,128)}, f32[3,6,256,256]{3,2,1,0:T(8,128)}, /*index=5*/s32[3,6]{1,0:T(4,128)}, ...), branch_computations={%region_3.4_spmd, %region_4.5_spmd, %region_5.6_spmd, %region_6.7_... | conditional | flops 12079595520 | bytes 140069360 | solution.py:416
  80.3 0.1 copy.68
  80.4 0.7 slice_bitcast_fusion.36
  81.1 0.6 reshape.317.own_ref
  81.7 0.0 copy-start.9
  81.7 0.0 copy-start.22
  81.7 0.0 slice-start.18
  81.7 264.5 %pack.22 = (f32[23,256,256]{2,1,0:T(8,128)}, f32[23,256,256]{2,1,0:T(8,128)}) custom-call(s32[42]{0:T(128)} %reshape.317.own_ref, s32[36]{0:T(128)} %get-tuple-element.1021.forth_ref, s32[36]{0:T(128)} %get-tuple-element.1020.back_ref, f32[18,256,256]{2,1,0:T(8,128)} %bitcast.242, f32[18,256,256]{2,1,0:T(8,128)} %bitcast.204), custom_call_target="tpu_custom_call" | custom-call | tf_op jit(solution)/shard_map/cond/branch_9_fun/pack/pallas_call | solution.py:137
  346.2 0.1 collective-permute-start.18
  346.2 5.3 collective-permute-start.19
  351.6 0.0 copy-done.9
  351.6 0.7 reshape.318.off_ref
  352.3 0.0 copy-done.22
  352.3 0.7 reshape.321.weight_ref
  352.9 0.0 slice-start.19
  352.9 31.6 %own_rows.22 = (f32[21,256,256]{2,1,0:T(8,128)}, bf16[36,256,256]{2,1,0:T(8,128)(2,1)}, bf16[36,256,256]{2,1,0:T(8,128)(2,1)}, s32[3,384]{1,0:T(4,128)}) custom-call(s32[42]{0:T(128)} %reshape.317.own_ref, s32[36]{0:T(128)} %get-tuple-element.1023.left_ref, s32[36]{0:T(128)} %get-tuple-element.1022.right_ref, s32[18]{0:T(128)} %reshape.318.off_ref, ...), custom_call_target="tpu_custom_call" | custom-call | flops 6039797760 | bytes 31457280 | tf_op jit(solution)/shard_map/cond/branch_9_fun/own_rows/pallas_call | solution.py:245
  384.5 92.4 %collective-permute-done.18.low_ref = f32[23,256,256]{2,1,0:T(8,128)} collective-permute-done((f32[23,256,256]{2,1,0:T(8,128)}, f32[23,256,256]{2,1,0:T(8,128)}, u32[]{:S(2)}, u32[]{:S(2)}) %collective-permute-start.18) | collective-permute-done | bytes 6029344 | tf_op jit(solution)/shard_map/cond/branch_9_fun/ppermute | solution.py:406
  476.9 127.6 %collective-permute-done.19.high_ref = f32[23,256,256]{2,1,0:T(8,128)} collective-permute-done((f32[23,256,256]{2,1,0:T(8,128)}, f32[23,256,256]{2,1,0:T(8,128)}, u32[]{:S(2)}, u32[]{:S(2)}) %collective-permute-start.19) | collective-permute-done | bytes 6029344 | tf_op jit(solution)/shard_map/cond/branch_9_fun/ppermute | solution.py:407
  604.5 0.0 slice-done.18
  604.5 0.0 slice-done.19
  604.5 26.5 %halo_rows.22 = (f32[18,256,256]{2,1,0:T(8,128)}, f32[1,1]{1,0:T(1,128)}) custom-call(s32[3,384]{1,0:T(4,128)} %get-tuple-element.557.lists_ref, s32[2]{0:T(128)S(1)} %get-tuple-element.558.counts_ref, s32[18]{0:T(128)} %reshape.318.off_ref, s32[18]{0:T(128)} %reshape.321.weight_ref, f32[23,256,256]{2,1,0:T(8,128)} %collective-permute-done.18.low_ref, ...), custom_call_target="tpu_custom_call" | custom-call | flops 6039797760 | bytes 31457280 | tf_op jit(solution)/shard_map/cond/branch_9_fun/halo_rows/pallas_call | solution.py:347
  631.3 40.7 %psum.7 = f32[]{:T(128)} all-reduce(f32[]{:T(128)} %bitcast.102), channel_id=1, replica_groups=mesh['row'=8,'col'=4] {'row','col'}, use_global_device_ids=true, to_apply=%region_16.17 | all-reduce | flops 1 | bytes 8 | tf_op jit(solution)/shard_map/psum | solution.py:421
  (6 shorter events, 0.0 us)
Async XLA Ops:
  81.7 269.9 %copy-start.9 = (s32[3,6]{1,0:T(4,128)S(1)}, s32[3,6]{1,0:T(4,128)}, u32[]{:S(2)}) copy-start(s32[3,6]{1,0:T(4,128)} %get-tuple-element.554) | copy-start | bytes 220 | tf_op jit(solution)/shard_map/cond
  81.7 270.6 %copy-start.22 = (s32[3,6]{1,0:T(4,128)S(1)}, s32[3,6]{1,0:T(4,128)}, u32[]{:S(2)}) copy-start(s32[3,6]{1,0:T(4,128)} %get-tuple-element.559) | copy-start | bytes 220 | tf_op jit(solution)/shard_map/cond
  81.7 522.9 %slice-start.18 = ((s8[4718592]{0:T(1024)(128)(4,1)}), s8[524288]{0:T(1024)(128)(4,1)S(1)}, s32[]{:S(2)}) async-start(s8[4718592]{0:T(1024)(128)(4,1)} %bitcast.206), calls=%async_computation.18 | async-start | bytes 1048576 | tf_op jit(solution)/shard_map/cond
  346.2 130.7 %collective-permute-start.18 = (f32[23,256,256]{2,1,0:T(8,128)}, f32[23,256,256]{2,1,0:T(8,128)}, u32[]{:S(2)}, u32[]{:S(2)}) collective-permute-start(f32[23,256,256]{2,1,0:T(8,128)} %get-tuple-element.560), channel_id=1, source_target_pairs={{0,1},{1,2},{2,3},{3,4},{4,5},{5,6},{6,7},{7,8},{8,9},{9,10},{10,1... | collective-permute-start | bytes 18087944 | tf_op jit(solution)/shard_map/cond/branch_9_fun/ppermute | solution.py:406
  346.2 258.3 %collective-permute-start.19 = (f32[23,256,256]{2,1,0:T(8,128)}, f32[23,256,256]{2,1,0:T(8,128)}, u32[]{:S(2)}, u32[]{:S(2)}) collective-permute-start(f32[23,256,256]{2,1,0:T(8,128)} %get-tuple-element.561), channel_id=1, source_target_pairs={{1,0},{2,1},{3,2},{4,3},{5,4},{6,5},{7,6},{8,7},{9,8},{10,9},{11,1... | collective-permute-start | bytes 18087944 | tf_op jit(solution)/shard_map/cond/branch_9_fun/ppermute | solution.py:407
  352.9 251.6 %slice-start.19 = ((s8[4718592]{0:T(1024)(128)(4,1)}), s8[4194304]{0:T(1024)(128)(4,1)S(1)}, s32[]{:S(2)}) async-start(s8[4718592]{0:T(1024)(128)(4,1)} %bitcast.206), calls=%async_computation.19 | async-start | bytes 8388608 | tf_op jit(solution)/shard_map/cond

commit v2 on v1

v2 whole, which is shorter than its diff:
```python
import functools

import jax
import jax.numpy as jnp
from jax import lax
from jax.experimental import pallas as pl
from jax.experimental.pallas import tpu as pltpu
from jax.sharding import PartitionSpec as P

HALF = 3
WIDTH = 2 * HALF + 1
WIN = 2 * HALF
AXES = ("row", "col")
VMEM_LIMIT = 58 * 1024 * 1024
F32 = jnp.float32
BF16 = jnp.bfloat16
I32 = jnp.int32


def need_cells(side):
    base = 0 if side == 0 else HALF
    return [
        (t, k, j)
        for t in range(2)
        for k in range(HALF)
        for j in range(WIN)
        if abs(j - (base + k)) <= HALF
    ]


def cell(t, k, j):
    return (t * HALF + k) * WIN + j


CELLS = 2 * HALF * WIN
RESULTS = HALF * WIN
CELL_ROW = (0, CELLS)
RESULT_ROW = (2 * CELLS, 2 * CELLS + RESULTS)
BIT_ROW = 2 * CELLS + 2 * RESULTS
COUNT_ROW = (BIT_ROW + WIN, BIT_ROW + WIN + 1)
CROSS_ROW = (BIT_ROW + WIN + 2, BIT_ROW + WIN + 3)
SUM_ROW = (BIT_ROW + WIN + 4, BIT_ROW + WIN + 5)
TOP_ROW = BIT_ROW + WIN + 6
PLAN_ROWS = 128


def split_room(room):
    first, last = (room + 1) // 2, room * 3 // 8
    return first, room - first - last, last


def room_for_sums(sums):
    return ((8 * sums + 2) * 171) >> 9


def either(flags):
    return functools.reduce(jnp.bitwise_or, flags)


def plan_kernel(slots, me_ref, meta_ref, out_ref, table):
    n = meta_ref.shape[-1]
    fields = 3 * slots

    def row(i, f):
        source, r = (0, i) if i < HALF else (1, i - HALF)
        at = r * fields + f
        return meta_ref[source, at : at + 1, :]

    one = jnp.ones((1, n), I32)
    zero = jnp.zeros((1, n), I32)
    live = [{}, {}]
    kept, shown = {}, {}
    for i in range(WIN):
        offs = [row(i, 2 * slots + s) for s in range(slots)]
        flags = [[jnp.where(row(i, t * slots + s) == 1, one, zero) for s in range(slots)] for t in range(2)]
        for j in range(WIN):
            d = j - i
            if abs(d) > HALF:
                continue
            here = [jnp.where(o == d, one, zero) for o in offs]
            kept[i, j] = either(here)
            shown[i, j] = one if d == 0 else kept[i, j]
            for t in range(2):
                live[t][i, j] = either([h & f for h, f in zip(here, flags[t])])

    def near(*pairs):
        return all(abs(p - q) <= HALF for p, q in pairs)

    as_left = {}
    for side in range(2):
        base, other = (0, HALF) if side == 0 else (HALF, 0)
        for t, k, j in need_cells(side):
            if other <= j < other + HALF:
                ends = [
                    live[1 - t][j, e] & shown[base + k, e] for e in range(WIN) if near((e, j), (e, base + k))
                ]
                as_left[side, t, k, j] = live[t][base + k, j] & either(ends)
    sums = {}
    for side in range(2):
        base, other = (0, HALF) if side == 0 else (HALF, 0)
        for i in range(other, other + HALF):
            for j in range(WIN):
                if near((i, j)):
                    terms = [
                        live[t][i, k] & live[1 - t][k, j]
                        for t in range(2)
                        for k in range(base, base + HALF)
                        if near((i, k), (k, j))
                    ]
                    if terms:
                        sums[side, i, j] = kept[i, j] & either(terms)

    def visit(bits, on_cell, on_sum):
        for side in range(2):
            base, other = (0, HALF) if side == 0 else (HALF, 0)

            def is_cross(spec):
                return other <= spec[2] < other + HALF

            for spec in sorted(need_cells(side), key=lambda c: not is_cross(c)):
                t, k, j = spec
                kk = base + k
                users = [
                    live[1 - t][i, kk] & shown[i, j] & (1 - bits[i])
                    for i in range(other, other + HALF)
                    if near((i, kk), (i, j))
                ]
                need = either(users) & live[t][kk, j]
                if is_cross(spec):
                    need = need | (bits[kk] & as_left[side, t, k, j])
                on_cell(side, spec, is_cross(spec), need)
            for i in range(other, other + HALF):
                for j in range(WIN):
                    if (side, i, j) in sums:
                        on_sum(side, i - other, j, sums[side, i, j] & bits[i])

    trials = 2**WIN
    trial = lax.broadcasted_iota(I32, (trials, n), 0)
    totals = {}

    def tally(name, side, value):
        totals[name, side] = totals[name, side] + value if (name, side) in totals else value

    def count_cell(side, spec, cross, need):
        tally("all", side, need)
        if cross:
            tally("cross", side, need)

    visit(
        [(trial >> i) & 1 for i in range(WIN)],
        count_cell,
        lambda side, i, j, need: tally("sum", side, need),
    )
    cost = jnp.zeros((trials, n), I32)
    load = jnp.zeros((trials, n), I32)
    for side in range(2):
        both = totals["all", side] + totals["sum", side]
        load = load + both
        cost = jnp.maximum(cost, both)
        cost = jnp.maximum(cost, 2 * totals["cross", side] - 1)
        cost = jnp.maximum(cost, room_for_sums(totals["sum", side]))
    score = ((cost * 256 + load) * trials + trial).astype(F32)
    best = jnp.min(score, axis=0, keepdims=True)
    best = best.astype(I32)
    bits = [(best >> i) & 1 for i in range(WIN)]
    top = jnp.max((best >> (8 + WIN)).astype(F32), axis=1, keepdims=True).astype(I32)

    table[...] = jnp.full(table.shape, -1, I32)

    def put(at, value):
        table[at : at + 1, :] = value

    counts = {key: zero for key in [(name, side) for name in ("all", "cross", "sum") for side in range(2)]}

    def place_cell(side, spec, cross, need):
        put(CELL_ROW[side] + cell(*spec), jnp.where(need == 1, counts["all", side], -one))
        counts["all", side] = counts["all", side] + need
        if cross:
            counts["cross", side] = counts["cross", side] + need

    def place_sum(side, i, j, need):
        put(RESULT_ROW[side] + i * WIN + j, jnp.where(need == 1, counts["sum", side], -one))
        counts["sum", side] = counts["sum", side] + need

    visit(bits, place_cell, place_sum)
    for i in range(WIN):
        put(BIT_ROW + i, bits[i])
    for side in range(2):
        put(COUNT_ROW[side], counts["all", side])
        put(CROSS_ROW[side], counts["cross", side])
        put(SUM_ROW[side], counts["sum", side])
    put(TOP_ROW, jnp.broadcast_to(top, (1, n)))

    me = me_ref[0]
    whole = table[...]
    lane = lax.broadcasted_iota(I32, whole.shape, 1)
    right = lax.rem(me + 1, n)
    first = jnp.sum(jnp.where(lane == me, whole, 0), axis=1, keepdims=True)
    second = jnp.sum(jnp.where(lane == right, whole, 0), axis=1, keepdims=True)
    out_lane = lax.broadcasted_iota(I32, out_ref.shape, 1)
    out_ref[...] = jnp.where(out_lane == 0, first, second)


def make_plan(meta, me, slots):
    n, rows = meta.shape[0], meta.shape[1]
    low = jnp.roll(meta[:, rows - HALF :], 1, axis=0).reshape(n, -1).T
    high = meta[:, :HALF].reshape(n, -1).T
    return pl.pallas_call(
        functools.partial(plan_kernel, slots),
        out_shape=jax.ShapeDtypeStruct((PLAN_ROWS, 128), I32),
        in_specs=[pl.BlockSpec(memory_space=pltpu.SMEM), pl.BlockSpec(memory_space=pltpu.VMEM)],
        out_specs=pl.BlockSpec(memory_space=pltpu.VMEM),
        scratch_shapes=[pltpu.VMEM((PLAN_ROWS, n), I32)],
        name="plan",
    )(me.reshape(1), jnp.stack([low, high]))


SMEM = pl.BlockSpec(memory_space=pltpu.SMEM)
VMEM = pl.BlockSpec(memory_space=pltpu.VMEM)
HBM = pl.BlockSpec(memory_space=pl.ANY)
SENT = 2 * HALF * WIN + 1


def over(count, act, begin=0):
    def step(i, carry):
        act(i)
        return carry

    lax.fori_loop(begin, count, step, 0)


def list_sent(rows, own_ref, left_ref, right_ref, sent_ref):
    for side, plan_ref in ((0, right_ref), (1, left_ref)):
        for t, k, j in need_cells(side):
            own_row = rows - HALF + k if side == 0 else k
            place = j - k + HALF if side == 0 else j - k
            at = plan_ref[CELL_ROW[side] + cell(t, k, j)]
            at = jnp.where(at >= 0, at, SENT - 1)
            sent_ref[side * SENT + at] = own_ref[(t * rows + own_row) * WIDTH + place]


class Carrier:
    def __init__(self, side, low, high, shift, sent_ref, x_ref, t_ref, out, held, sems_in, sems_out):
        self.side, self.low, self.count, self.shift = side, low, jnp.maximum(high - low, 0), shift
        self.sent_ref, self.sources, self.out, self.held = sent_ref, (x_ref, t_ref), out, held
        self.sems_in, self.sems_out = sems_in, sems_out

    def arrival(self, t, block, i):
        return pltpu.make_async_copy(self.sources[t].at[block], self.held.at[self.side, i], self.sems_in.at[self.side, i])

    def departure(self, i):
        target = self.out.at[self.shift + i]
        return pltpu.make_async_copy(self.held.at[self.side, i], target, self.sems_out.at[self.side, i])

    def begin(self):
        stored = self.sources[0].shape[0]

        def act(i):
            block = self.sent_ref[self.side * SENT + self.low + i]
            for t in range(2):

                @pl.when((block >= stored) == (t == 1))
                def _():
                    self.arrival(t, block - t * stored, i).start()

        over(self.count, act)

    def onward(self):
        def act(i):
            self.arrival(0, 0, i).wait()
            self.departure(i).start()

        over(self.count, act)

    def end(self):
        over(self.count, lambda i: self.departure(i).wait())


def pack_kernel(rows, low, high, own_ref, left_ref, right_ref, x_ref, t_ref, forth_out, back_out, sent_ref, held, sems_in, sems_out):
    list_sent(rows, own_ref, left_ref, right_ref, sent_ref)
    carriers = [
        Carrier(side, low, jnp.minimum(count, high), 0, sent_ref, x_ref, t_ref, out, held, sems_in, sems_out)
        for side, count, out in (
            (0, right_ref[COUNT_ROW[0]], forth_out),
            (1, left_ref[COUNT_ROW[1]], back_out),
        )
    ]
    for carrier in carriers:
        carrier.begin()
    for carrier in carriers:
        carrier.onward()
    for carrier in carriers:
        carrier.end()


def pack(own, left, right, x, t, low, high, rows):
    block = x.shape[1:]
    room = high - low
    shape = jax.ShapeDtypeStruct((room,) + block, F32)
    return pl.pallas_call(
        functools.partial(pack_kernel, rows, low, high),
        out_shape=(shape, shape, jax.ShapeDtypeStruct((2 * SENT,), I32)),
        in_specs=[SMEM] * 3 + [HBM] * 2,
        out_specs=(HBM, HBM, SMEM),
        scratch_shapes=[
            pltpu.VMEM((2, room) + block, F32),
            pltpu.SemaphoreType.DMA((2, room)),
            pltpu.SemaphoreType.DMA((2, room)),
        ],
        compiler_params=pltpu.CompilerParams(vmem_limit_bytes=VMEM_LIMIT),
        name="pack",
    )(own, left, right, x, t)


def halves(values):
    high = values.astype(BF16)
    return high, (values - high.astype(F32)).astype(BF16)


STRIPE = 32


def stripes(block, act):
    over(block[0] // STRIPE, lambda i: act(pl.ds(pl.multiple_of(i * STRIPE, STRIPE), STRIPE)))


def split_block(source, at, high_ref, low_ref, to):
    def act(part):
        high_ref[to, part, :], low_ref[to, part, :] = halves(source[at, part, :])

    stripes(source.shape[1:], act)


def add_product(total, at, sign, lh, ll, i, rh, rl, j):
    dot = functools.partial(jnp.dot, preferred_element_type=F32)
    half = total.shape[-2] // 2

    def act(h):
        part = pl.ds(pl.multiple_of(h * half, half), half)
        high, low = lh[i, part, :], ll[i, part, :]
        result = dot(high, rh[j]) + (dot(high, rl[j]) + dot(low, rh[j]))
        total[at, part, :] += result if sign == 1 else sign * result

    over(2, act)


OWN, FIRST, LAST, HELP = range(4)
LEFT, RIGHT, BEGIN = range(3)


def list_length(rows, slots):
    return -(-((rows * slots + rows) * 2 * WIDTH + 1) // 128) * 128


def own_kernel(
    rows, slots, room_a, room_c, room_b,
    own_ref, left_ref, right_ref, off_ref, x_ref, t_ref,
    part_ref, high_ref, low_ref, lists_ref, used_ref,
):
    stored = rows * slots
    outs = stored + rows
    early = room_a + room_c
    late = [left_ref[SUM_ROW[0]] - early, room_b + right_ref[SUM_ROW[1]] - early]

    def clear(i, carry):
        used_ref[i] = 0
        return carry

    lax.fori_loop(0, 2 * stored, clear, 0)

    def of_output(q, counts):
        is_diag = q >= stored
        row = jnp.where(is_diag, q - stored, lax.div(q, slots))
        d = jnp.where(is_diag, 0, off_ref[jnp.minimum(q, stored - 1)])
        has_zero = jnp.bool_(False)
        for s in range(slots):
            has_zero = has_zero | (off_ref[row * slots + s] == 0)
        wanted = jnp.logical_not(is_diag & has_zero)
        for which in (OWN, FIRST, LAST):
            lists_ref[which, BEGIN, q] = counts[which]
        low_row = row - (rows - HALF)
        left_open = (row < HALF) & (left_ref[BIT_ROW + HALF + jnp.minimum(row, HALF - 1)] == 0)
        right_open = (low_row >= 0) & (right_ref[BIT_ROW + jnp.maximum(low_row, 0)] == 0)
        column = row + d

        def of_term(m, counts):
            t = lax.rem(m, 2)
            e = lax.div(m, 2) - HALF
            k = row + e
            place = d - e + HALF
            ok = wanted & (place >= 0) & (place < WIDTH)
            left = own_ref[(t * rows + row) * WIDTH + e + HALF]
            ok = ok & (left >= 0)
            is_own = ok & (k >= 0) & (k < rows)
            is_low = ok & (k < 0) & left_open
            is_high = ok & (k >= rows) & right_open
            own_block = own_ref[jnp.where(is_own, ((1 - t) * rows + k) * WIDTH + place, 0)]
            low_at = ((1 - t) * HALF + k + HALF) * WIN + column + HALF
            low_block = left_ref[CELL_ROW[0] + jnp.where(is_low, low_at, 0)]
            high_at = ((1 - t) * HALF + k - rows) * WIN + column - rows + HALF
            high_block = right_ref[CELL_ROW[1] + jnp.where(is_high, high_at, 0)]
            far_block = jnp.where(is_low, low_block, high_block)
            far_ok = (is_low | is_high) & (far_block >= 0)
            own_count, first_count, last_count = counts
            lists_ref[OWN, LEFT, own_count] = left
            lists_ref[OWN, RIGHT, own_count] = own_block
            own_count = own_count + jnp.where(is_own & (own_block >= 0), 1, 0)
            lists_ref[FIRST, LEFT, first_count] = left
            lists_ref[FIRST, RIGHT, first_count] = far_block + jnp.where(is_low, 0, early)
            first_count = first_count + jnp.where(far_ok & (far_block < early), 1, 0)
            lists_ref[LAST, LEFT, last_count] = left
            lists_ref[LAST, RIGHT, last_count] = far_block + jnp.where(is_low, late[0], late[1])
            is_last = far_ok & (far_block >= early)
            last_count = last_count + jnp.where(is_last, 1, 0)

            @pl.when(is_last)
            def _():
                used_ref[left] = 1

            return own_count, first_count, last_count

        return lax.fori_loop(0, 2 * WIDTH, of_term, counts)

    ends = lax.fori_loop(0, outs, of_output, (jnp.int32(0),) * 3)
    for which in (OWN, FIRST, LAST):
        lists_ref[which, BEGIN, outs] = ends[which]

    count = jnp.int32(0)
    for side, plan_ref in ((0, right_ref), (1, left_ref)):
        base, other = (0, HALF) if side == 0 else (HALF, 0)
        shift = rows - HALF if side == 0 else 0

        def of_sum(q, count):
            i = lax.div(q, WIN)
            j = lax.rem(q, WIN)
            open_row = plan_ref[BIT_ROW + other + i] == 1
            shown = (plan_ref[RESULT_ROW[side] + q] >= 0) | (j == other + i)
            open_row = open_row & shown
            lists_ref[HELP, BEGIN, side * RESULTS + q] = count

            def of_term(m, count):
                t = lax.rem(m, 2)
                k = lax.div(m, 2)
                reach = j - (base + k)
                ok = open_row & (reach >= -HALF) & (reach <= HALF)
                across = other + i - (base + k)
                ok = ok & (across >= -HALF) & (across <= HALF)
                left = plan_ref[CELL_ROW[1 - side] + (t * HALF + i) * WIN + base + k]
                right_at = jnp.where(ok, ((1 - t) * rows + shift + k) * WIDTH + reach + HALF, 0)
                right = own_ref[right_at]
                lists_ref[HELP, LEFT, count] = left + (room_a if side == 0 else 0)
                lists_ref[HELP, RIGHT, count] = right
                return count + jnp.where(ok & (left >= 0) & (right >= 0), 1, 0)

            return lax.fori_loop(0, 2 * HALF, of_term, count)

        count = lax.fori_loop(0, RESULTS, of_sum, count)
    lists_ref[HELP, BEGIN, 2 * RESULTS] = count

    def split(i, carry):
        for t, source in enumerate((x_ref, t_ref)):
            split_block(source, i, high_ref, low_ref, t * stored + i)
        return carry

    lax.fori_loop(0, stored, split, 0)

    def compute(q, carry):
        part_ref[q] = jnp.zeros(part_ref.shape[1:], F32)

        def term(m, carry):
            left = lists_ref[OWN, LEFT, m]
            right = lists_ref[OWN, RIGHT, m]
            add_product(part_ref, q, 1, high_ref, low_ref, left, high_ref, low_ref, right)
            return carry

        return lax.fori_loop(lists_ref[OWN, BEGIN, q], lists_ref[OWN, BEGIN, q + 1], term, carry)

    lax.fori_loop(0, outs, compute, 0)


def own_part(own, left, right, offsets, x, t, room_a, room_c, room_b, rows, slots):
    stored = rows * slots
    block = x.shape[1:]
    length = list_length(rows, slots)
    return pl.pallas_call(
        functools.partial(own_kernel, rows, slots, room_a, room_c, room_b),
        out_shape=(
            jax.ShapeDtypeStruct((stored + rows,) + block, F32),
            jax.ShapeDtypeStruct((2 * stored,) + block, BF16),
            jax.ShapeDtypeStruct((2 * stored,) + block, BF16),
            jax.ShapeDtypeStruct((4, 3, length), I32),
            jax.ShapeDtypeStruct((2 * stored,), I32),
        ),
        in_specs=[SMEM] * 4 + [VMEM] * 2,
        out_specs=(VMEM, VMEM, VMEM, SMEM, SMEM),
        compiler_params=pltpu.CompilerParams(vmem_limit_bytes=VMEM_LIMIT),
        cost_estimate=pl.CostEstimate(
            flops=2**20, bytes_accessed=2**16, transcendentals=0
        ),
        name="own_rows",
    )(own, left, right, offsets, x, t)


def convert_blocks(source, count, shift, far_high, far_low, stage, stage_sems):
    depth = stage.shape[0]

    def fetch(i):
        slot = lax.rem(i, depth)
        return pltpu.make_async_copy(source.at[i], stage.at[slot], stage_sems.at[slot])

    for i in range(depth - 1):

        @pl.when(i < count)
        def _():
            fetch(i).start()

    def convert(i, carry):
        @pl.when(i + depth - 1 < count)
        def _():
            fetch(i + depth - 1).start()

        fetch(i).wait()
        split_block(stage, lax.rem(i, depth), far_high, far_low, shift + i)
        return carry

    lax.fori_loop(0, count, convert, 0)


def trace_of(ref, at):
    side = ref.shape[-1]

    def stripe(i, total):
        first = pl.multiple_of(i * STRIPE, STRIPE)
        row = lax.broadcasted_iota(I32, (STRIPE, side), 0) + first
        column = lax.broadcasted_iota(I32, (STRIPE, side), 1)
        return total + jnp.where(row == column, ref[at, pl.ds(first, STRIPE), :], 0.0)

    return jnp.sum(lax.fori_loop(0, side // STRIPE, stripe, jnp.zeros((STRIPE, side), F32)))


def help_kernel(
    rows, room_a, early, room_b,
    sent_ref, left_ref, right_ref, lists_ref,
    low_ref, high_ref, own_high_ref, own_low_ref, x_ref, t_ref,
    forth_out, back_out, trace_ref,
    stage, far_high, far_low, own_high, own_low, sums, held, stage_sems, sems, sum_sems, sems_in, sems_out,
):
    outs = (forth_out, back_out)
    copies = [
        pltpu.make_async_copy(source, target, sems.at[i])
        for i, (source, target) in enumerate(((own_high_ref, own_high), (own_low_ref, own_low)))
    ]
    helps = lists_ref[HELP, BEGIN, 2 * RESULTS] > 0

    @pl.when(helps)
    def _():
        for copy in copies:
            copy.start()

    shifts = (right_ref[SUM_ROW[0]], left_ref[SUM_ROW[1]])
    carriers = [
        Carrier(side, early, count, shifts[side], sent_ref, x_ref, t_ref, outs[side], held, sems_in, sems_out)
        for side, count in ((0, right_ref[COUNT_ROW[0]]), (1, left_ref[COUNT_ROW[1]]))
    ]
    for carrier in carriers:
        carrier.begin()
    trace_ref[0, 0] = jnp.float32(0)

    @pl.when(helps)
    def _():
        convert_blocks(low_ref, left_ref[CROSS_ROW[0]], 0, far_high, far_low, stage, stage_sems)
        convert_blocks(high_ref, right_ref[CROSS_ROW[1]], room_a, far_high, far_low, stage, stage_sems)
        for copy in copies:
            copy.wait()

    for carrier in carriers:
        carrier.onward()
    for side, plan_ref in ((0, right_ref), (1, left_ref)):
        other = HALF if side == 0 else 0

        def compute(q, carry):
            begin_at = lists_ref[HELP, BEGIN, side * RESULTS + q]
            end_at = lists_ref[HELP, BEGIN, side * RESULTS + q + 1]
            at = plan_ref[RESULT_ROW[side] + q]

            @pl.when(end_at > begin_at)
            def _():
                slot = jnp.where(at >= 0, at, room_b)
                sums[side, slot] = jnp.zeros(sums.shape[2:], F32)

                def term(m, carry):
                    left = lists_ref[HELP, LEFT, m]
                    right = lists_ref[HELP, RIGHT, m]
                    add_product(sums.at[side], slot, 1, far_high, far_low, left, own_high, own_low, right)
                    return carry

                lax.fori_loop(begin_at, end_at, term, 0)

                @pl.when(at >= 0)
                def _():
                    pltpu.make_async_copy(sums.at[side, slot], outs[side].at[slot], sum_sems.at[side, slot]).start()

                @pl.when(lax.rem(q, WIN) == other + lax.div(q, WIN))
                def _():
                    trace_ref[0, 0] += trace_of(sums.at[side], slot)

            return carry

        lax.fori_loop(0, RESULTS, compute, 0)
    for side in range(2):

        def finish(i, carry):
            pltpu.make_async_copy(sums.at[side, i], outs[side].at[i], sum_sems.at[side, i]).wait()
            return carry

        lax.fori_loop(0, shifts[side], finish, 0)
    for carrier in carriers:
        carrier.end()


def help_part(sent, left, right, lists, low, high, own_high, own_low, x, t, early, room_b, rows):
    room_a = low.shape[0]
    block = x.shape[1:]
    stored = x.shape[0]
    shape = jax.ShapeDtypeStruct((room_b,) + block, F32)
    return pl.pallas_call(
        functools.partial(help_kernel, rows, room_a, early, room_b),
        out_shape=(shape, shape, jax.ShapeDtypeStruct((1, 1), F32)),
        in_specs=[SMEM] * 4 + [HBM] * 6,
        out_specs=(HBM, HBM, SMEM),
        scratch_shapes=[
            pltpu.VMEM((4,) + block, F32),
            pltpu.VMEM((2 * room_a,) + block, BF16),
            pltpu.VMEM((2 * room_a,) + block, BF16),
            pltpu.VMEM((2 * stored,) + block, BF16),
            pltpu.VMEM((2 * stored,) + block, BF16),
            pltpu.VMEM((2, room_b + 1) + block, F32),
            pltpu.VMEM((2, room_b) + block, F32),
            pltpu.SemaphoreType.DMA((4,)),
            pltpu.SemaphoreType.DMA((2,)),
            pltpu.SemaphoreType.DMA((2, room_b)),
            pltpu.SemaphoreType.DMA((2, room_b)),
            pltpu.SemaphoreType.DMA((2, room_b)),
        ],
        compiler_params=pltpu.CompilerParams(vmem_limit_bytes=VMEM_LIMIT),
        cost_estimate=pl.CostEstimate(
            flops=2**20, bytes_accessed=2**16, transcendentals=0
        ),
        name="help_rows",
)(sent, left, right, lists, low, high, own_high, own_low, x, t)


def first_kernel(
    rows, slots, room_a, room_c,
    lists_ref, left_ref, right_ref, off_ref, weight_ref,
    low_ref, high_ref, low_ref_2, high_ref_2, own_high_ref, own_low_ref, part_ref, t_ref,
    out_ref, trace_ref,
    stage, far_high, far_low, own_high, own_low, total, tangent, stage_sems, sems,
):
    stored = rows * slots
    outs = stored + rows
    copies = [
        pltpu.make_async_copy(source, target, sems.at[i])
        for i, (source, target) in enumerate(
            ((own_high_ref, own_high), (own_low_ref, own_low), (part_ref, total), (t_ref, tangent))
        )
    ]
    for copy in copies:
        copy.start()
    early = room_a + room_c
    for side, (source, source_2, plan_ref) in enumerate(
        ((low_ref, low_ref_2, left_ref), (high_ref, high_ref_2, right_ref))
    ):
        whole = plan_ref[COUNT_ROW[side]]
        convert_blocks(source, jnp.minimum(whole, room_a), side * early, far_high, far_low, stage, stage_sems)
        count = jnp.maximum(jnp.minimum(whole, early) - room_a, 0)
        convert_blocks(source_2, count, side * early + room_a, far_high, far_low, stage, stage_sems)
    for copy in copies:
        copy.wait()

    trace_ref[0, 0] = jnp.float32(0)

    def compute(q, carry):
        def term(m, carry):
            left = lists_ref[FIRST, LEFT, m]
            right = lists_ref[FIRST, RIGHT, m]
            add_product(total, q, 1, own_high, own_low, left, far_high, far_low, right)
            return carry

        lax.fori_loop(lists_ref[FIRST, BEGIN, q], lists_ref[FIRST, BEGIN, q + 1], term, 0)

        @pl.when(q < stored)
        def _():
            at = jnp.minimum(q, stored - 1)
            scale = 1.5 * weight_ref[at].astype(F32)

            def act(part):
                out_ref[at, part, :] = scale * tangent[at, part, :] - 0.5 * total[q, part, :]

            stripes(total.shape[1:], act)

        @pl.when((q >= stored) | (off_ref[jnp.minimum(q, stored - 1)] == 0))
        def _():
            trace_ref[0, 0] += trace_of(total, q)

        return carry

    lax.fori_loop(0, outs, compute, 0)


def first_part(lists, left, right, offsets, weights, low, high, low_2, high_2, own_high, own_low, part, t, rows, slots):
    room_a, room_c = low.shape[0], low_2.shape[0]
    room = room_a + room_c
    stored = rows * slots
    block = t.shape[1:]
    return pl.pallas_call(
        functools.partial(first_kernel, rows, slots, room_a, room_c),
        out_shape=(
            jax.ShapeDtypeStruct((stored,) + block, F32),
            jax.ShapeDtypeStruct((1, 1), F32),
        ),
        in_specs=[SMEM] * 5 + [HBM] * 8,
        out_specs=(VMEM, SMEM),
        scratch_shapes=[
            pltpu.VMEM((4,) + block, F32),
            pltpu.VMEM((2 * room,) + block, BF16),
            pltpu.VMEM((2 * room,) + block, BF16),
            pltpu.VMEM((2 * stored,) + block, BF16),
            pltpu.VMEM((2 * stored,) + block, BF16),
            pltpu.VMEM((stored + rows,) + block, F32),
            pltpu.VMEM((stored,) + block, F32),
            pltpu.SemaphoreType.DMA((4,)),
            pltpu.SemaphoreType.DMA((4,)),
        ],
        compiler_params=pltpu.CompilerParams(vmem_limit_bytes=VMEM_LIMIT),
        cost_estimate=pl.CostEstimate(
            flops=2**20, bytes_accessed=2**16, transcendentals=0
        ),
        name="first_halo",
    )(lists, left, right, offsets, weights, low, high, low_2, high_2, own_high, own_low, part, t)


def last_kernel(
    rows, slots, early, room_b,
    lists_ref, used_ref, left_ref, right_ref, off_ref,
    low_ref, high_ref, own_high_ref, own_low_ref, given_ref,
    out_ref,
    got, far_high, far_low, own_high, own_low, held, got_sems, own_sems, in_sems, out_sems,
):
    stored = rows * slots
    plans = (left_ref, right_ref)
    sources = (low_ref, high_ref)
    sum_counts = [plans[side][SUM_ROW[side]] for side in range(2)]
    counts = [
        sum_counts[side] + jnp.maximum(plans[side][COUNT_ROW[side]] - early, 0) for side in range(2)
    ]

    def fetch(side, i):
        return pltpu.make_async_copy(sources[side].at[i], got.at[side, i], got_sems.at[side, i])

    def places(q):
        row = lax.div(q, slots)
        column = row + off_ref[q]
        low_ok = (row < HALF) & (column < HALF)
        low_at = left_ref[RESULT_ROW[0] + jnp.where(low_ok, row * WIN + column + HALF, 0)]
        low_at = jnp.where(low_ok, low_at, -1)
        base = rows - HALF
        high_ok = (row >= base) & (column >= base)
        high_at = right_ref[RESULT_ROW[1] + jnp.where(high_ok, (row - base) * WIN + column - base, 0)]
        high_at = jnp.where(high_ok, high_at, -1)
        begin, end = lists_ref[LAST, BEGIN, q], lists_ref[LAST, BEGIN, q + 1]
        return low_at, high_at, begin, end

    def touched(q):
        low_at, high_at, begin, end = places(q)
        return (low_at >= 0) | (high_at >= 0) | (end > begin)

    def load(q):
        return pltpu.make_async_copy(given_ref.at[q], held.at[q], in_sems.at[q])

    def store(q):
        return pltpu.make_async_copy(held.at[q], out_ref.at[q], out_sems.at[q])

    for side in range(2):
        over(counts[side], lambda i, side=side: fetch(side, i).start())

    def when_touched(act):
        def step(q):
            @pl.when(touched(q))
            def _():
                act(q)

        return step

    over(stored, when_touched(lambda q: load(q).start()))

    def own_copies(i):
        return (
            pltpu.make_async_copy(own_high_ref.at[i], own_high.at[i], own_sems.at[0, i]),
            pltpu.make_async_copy(own_low_ref.at[i], own_low.at[i], own_sems.at[1, i]),
        )

    def on_used(act):
        def step(i):
            @pl.when(used_ref[i] == 1)
            def _():
                for copy in own_copies(i):
                    act(copy)

        over(2 * stored, step)

    on_used(lambda copy: copy.start())
    for side in range(2):
        over(counts[side], lambda i, side=side: fetch(side, i).wait())

        def convert(i, carry):
            split_block(got.at[side], i, far_high, far_low, side * room_b + i)
            return carry

        lax.fori_loop(sum_counts[side], counts[side], convert, 0)
    on_used(lambda copy: copy.wait())

    def compute(q):
        low_at, high_at, begin, end = places(q)
        load(q).wait()

        @pl.when(low_at >= 0)
        def _():
            held[q] -= 0.5 * got[0, low_at]

        @pl.when(high_at >= 0)
        def _():
            held[q] -= 0.5 * got[1, high_at]

        def term(m, carry):
            left = lists_ref[LAST, LEFT, m]
            right = lists_ref[LAST, RIGHT, m]
            add_product(held, q, -0.5, own_high, own_low, left, far_high, far_low, right)
            return carry

        lax.fori_loop(begin, end, term, 0)
        store(q).start()

    over(stored, when_touched(compute))
    over(stored, when_touched(lambda q: store(q).wait()))


def last_part(lists, used, left, right, offsets, low, high, own_high, own_low, given, early, rows, slots):
    room_b = low.shape[0]
    stored = rows * slots
    block = given.shape[1:]
    return pl.pallas_call(
        functools.partial(last_kernel, rows, slots, early, room_b),
        out_shape=jax.ShapeDtypeStruct(given.shape, F32),
        in_specs=[SMEM] * 5 + [HBM] * 5,
        out_specs=HBM,
        input_output_aliases={9: 0},
        scratch_shapes=[
            pltpu.VMEM((2, room_b) + block, F32),
            pltpu.VMEM((2 * room_b,) + block, BF16),
            pltpu.VMEM((2 * room_b,) + block, BF16),
            pltpu.VMEM((2 * stored,) + block, BF16),
            pltpu.VMEM((2 * stored,) + block, BF16),
            pltpu.VMEM((stored,) + block, F32),
            pltpu.SemaphoreType.DMA((2, room_b)),
            pltpu.SemaphoreType.DMA((2, 2 * stored)),
            pltpu.SemaphoreType.DMA((stored,)),
            pltpu.SemaphoreType.DMA((stored,)),
        ],
        compiler_params=pltpu.CompilerParams(vmem_limit_bytes=VMEM_LIMIT),
        cost_estimate=pl.CostEstimate(
            flops=2**20, bytes_accessed=2**16, transcendentals=0
        ),
        name="last_halo",
    )(lists, used, left, right, offsets, low, high, own_high, own_low, given)


def partners(value, n, step):
    return lax.ppermute(value, AXES, [(i, i ^ step) for i in range(n)])


def steps_of(n):
    step = 1
    while step < n:
        yield (step, 2 * step, 3 * step) if 2 * step < n else (step,)
        step *= 4


def gather_all(value, n):
    if n & (n - 1):
        return lax.all_gather(value, AXES)
    value = value[None]
    for steps in steps_of(n):
        value = jnp.concatenate([value] + [partners(value, n, step) for step in steps])
    me = lax.axis_index(AXES)
    step = 1
    while step < n:
        pairs = value.reshape((n // (2 * step), 2, step) + value.shape[1:])
        value = jnp.where((me // step) % 2 == 0, pairs, pairs[:, ::-1]).reshape(value.shape)
        step *= 2
    return value


def sum_all(value, n):
    if n & (n - 1):
        return lax.psum(value, AXES)
    for steps in steps_of(n):
        others = [partners(value, n, step) for step in steps]
        value = value + others[0]
        if len(others) > 1:
            value = value + (others[1] + others[2])
    return value


def body(density_blocks, density_live, tangent_blocks, tangent_live, block_offsets):
    rows, slots = density_live.shape
    block = density_blocks.shape[2:]
    n = lax.axis_size("row") * lax.axis_size("col")
    me = lax.axis_index(AXES).astype(I32)
    x = density_blocks.reshape((rows * slots,) + block)
    t = tangent_blocks.reshape((rows * slots,) + block)
    offsets = block_offsets.reshape(-1)
    weights = tangent_live.reshape(-1)

    meta = jnp.concatenate([density_live, tangent_live, block_offsets], axis=1)
    gathered = gather_all(meta, n)
    plan = make_plan(gathered, me, slots)
    left, right = plan[:, 0], plan[:, 1]

    index = jnp.arange(rows * slots, dtype=I32).reshape(rows, slots, 1)
    here = block_offsets[:, :, None] == jnp.arange(-HALF, HALF + 1, dtype=I32)
    own = jnp.stack(
        [
            jnp.max(jnp.where(here & (live == 1)[:, :, None], index + shift, -1), axis=1)
            for live, shift in ((density_live, 0), (tangent_live, rows * slots))
        ]
    ).reshape(-1)

    forward = [(i, (i + 1) % n) for i in range(n)]
    backward = [(b, a) for a, b in forward]

    def exchange(forth, back):
        return lax.ppermute(forth, AXES, forward), lax.ppermute(back, AXES, backward)

    def with_room(room, own, left, right, offsets, weights, x, t):
        room_a, room_c, room_b = split_room(room)
        early = room_a + room_c
        forth, back, sent = pack(own, left, right, x, t, 0, room_a, rows)
        low, high = exchange(forth, back)
        forth, back, _ = pack(own, left, right, x, t, room_a, early, rows)
        low_2, high_2 = exchange(forth, back)
        own, _, _ = lax.optimization_barrier((own, forth, back))
        part, own_high, own_low, lists, used = own_part(
            own, left, right, offsets, x, t, room_a, room_c, room_b, rows, slots
        )
        forth, back, help_trace = help_part(
            sent, left, right, lists, low, high, own_high, own_low, x, t, early, room_b, rows
        )
        forth, back, low_2, high_2 = lax.optimization_barrier((forth, back, low_2, high_2))
        last_low, last_high = exchange(forth, back)
        given, trace = first_part(
            lists, left, right, offsets, weights, low, high, low_2, high_2, own_high, own_low, part, t, rows, slots
        )
        trace = sum_all(trace + help_trace, n)
        out = last_part(
            lists, used, left, right, offsets, last_low, last_high, own_high, own_low, given, early, rows, slots
        )
        return out, trace

    worst = len(need_cells(0))
    rooms = [r for r in (12, 13, 14, 15, 16, 17, 18, 19, 20, 22, 25) if r < worst] + [worst]
    choice = jnp.sum((left[TOP_ROW] > jnp.array(rooms[:-1], I32)).astype(I32))
    out, trace = lax.switch(
        choice,
        [functools.partial(with_room, room) for room in rooms],
        own, left, right, offsets, weights, x, t,
    )
    mean_trace = trace[0, 0] / (rows * n)
    return out.reshape(tangent_blocks.shape), mean_trace


def solution(mesh):
    return jax.shard_map(
        body,
        mesh=mesh,
        in_specs=(
            P(AXES, None, None, None),
            P(AXES, None),
            P(AXES, None, None, None),
            P(AXES, None),
            P(AXES, None),
        ),
        out_specs=(P(AXES, None, None, None), P()),
        check_vma=False,
    )
```

time: 667 us -> 261 us (0.39); the launches traced: 674 us -> 260 us
  Pallas kernels: 324 us -> 77.9 us
  waiting for transfers between devices: 220 us -> 82.8 us
  blocking collectives: 111 us -> 0 us
  starting transfers between devices: 5.39 us -> 74.7 us
  loops' own time: 0.58 us -> 10.5 us
    pallas_call x3 -> x6, Pallas kernels: 323 us -> 76.1 us  [the longest x1 37.7 us: own_part(): pl.pallas_call(functools.partial(own_kernel, rows, slots, room_a, room_c,...]
    ppermute x2 -> x20, waiting for transfers between devices: 220 us -> 82.8 us  [the longest x3 63.7 us: exchange(): lax.ppermute(back, AXES, backward)]
    all_gather x1 -> x0, blocking collectives: 70.1 us -> none  [body(): lax.all_gather(meta, AXES, tiled=True).reshape(n, rows, 3 * slots)]
    ppermute x2 -> x20, starting transfers between devices: 5.39 us -> 74.7 us  [the longest x14 58.6 us: partners(): return lax.ppermute(value, AXES, [(i, i ^ step) for i in range(n)])]
    psum x1 -> x0, blocking collectives: 40.7 us -> none  [body(): mean_trace = lax.psum(trace[0, 0], AXES) / (rows * n)]
    another operation x1, loops' own time: 0.58 us -> 10.5 us  [body(): lax.switch(choice, [functools.partial(with_room, room) for room in rooms]...]
  transfers between devices with their start and end apart: 2 -> 20, of which waited for: 2 -> 11; matrix products, arithmetic and copies ran while one was open for 0% -> 1% of each run, Pallas kernels for 5% -> 25%
where the time goes in v2:
time: 261 us; the launch traced here: 260 us
  waiting for transfers between devices  82.8 us (32%)
  Pallas kernels  77.9 us (30%)
  starting transfers between devices  74.7 us (29%)
  loops' own time  10.5 us (4%)
  local copies, waits for them, and re-layouts  5.92 us (2%)
  other arithmetic  4.93 us (2%)
  between operations  2.83 us (1%)
    ppermute x3, waiting for transfers between devices, exchange(): lax.ppermute(back, AXES, backward)  63.7 us
    ppermute x14, starting transfers between devices, partners(): return lax.ppermute(value, AXES, [(i, i ^ step) for i in range(n)])  58.6 us
    pallas_call x1, Pallas kernels, own_part(): pl.pallas_call(functools.partial(own_kernel, rows, slots, room_a, room_c,...  37.7 us
    pallas_call x1, Pallas kernels, first_part(): pl.pallas_call(functools.partial(first_kernel, rows, slots, room_a, room_...  23.3 us
    ppermute x3, starting transfers between devices, exchange(): lax.ppermute(back, AXES, backward)  14.5 us
    another operation x1, loops' own time, body(): lax.switch(choice, [functools.partial(with_room, room) for room in rooms]...  10.5 us
    ppermute x14, waiting for transfers between devices, partners(): return lax.ppermute(value, AXES, [(i, i ^ step) for i in range(n)])  10.5 us
    ppermute x3, waiting for transfers between devices, exchange(): lax.ppermute(forth, AXES, forward)  8.59 us
  transfers between devices with their start and end apart: 20, of which 11 were waited for; matrix products, arithmetic and copies ran while one was open for 1% of the time, Pallas kernels for 25%

profile of v2, /device:TPU:0, one launch (start us, length us, event | category | flops | bytes accessed | tf_op | source)
XLA Modules:
  0.0 259.6 jit_solution(10869851168737815106)
XLA Ops:
  0.6 0.8 constant_dynamic-update-slice_fusion.6
  1.4 5.0 %collective-permute-start.158 = (s32[1,3,18]{2,1,0:T(4,128)S(1)}, s32[1,3,18]{2,1,0:T(4,128)S(1)}, u32[]{:S(2)}, u32[]{:S(2)}) collective-permute-start(s32[1,3,18]{2,1,0:T(4,128)S(1)} %get-tuple-element.993), channel_id=1, source_target_pairs={{0,3},{1,2},{2,1},{3,0},{4,7},{5,6},{6,5},{7,4},{8,11},{9,10},{10,... | collective-permute-start | bytes 656 | tf_op jit(solution)/shard_map/ppermute | solution.py:879
  6.5 0.0 collective-permute-start.157
  6.5 0.6 collective-permute-start.156
  7.1 0.7 broadcast_compare_fusion
  7.8 0.8 select_reduce_fusion.1
  8.6 0.0 collective-permute-done.158
  8.6 2.3 collective-permute-done.157
  11.0 0.0 collective-permute-done.156
  11.0 0.1 collective-permute-start.161
  11.0 1.6 collective-permute-start.160
  12.6 0.3 collective-permute-start.159
  12.9 0.9 collective-permute-done.159
  13.8 1.0 collective-permute-done.160
  14.8 0.0 collective-permute-done.161
  14.8 1.6 collective-permute-start.162
  16.4 2.4 collective-permute-done.162
  18.8 0.1 rev.16
  19.0 0.1 rev.17
  19.2 0.1 copy.159
  19.3 0.1 copy.144
  19.4 0.1 reshape.303
  19.5 0.6 pad_add_fusion.meta_ref
  20.2 1.8 plan.1
  22.0 0.5 slice.116
  22.5 1.9 fusion
  25.1 233.2 %conditional.1 = (f32[3,6,256,256]{3,2,1,0:T(8,128)}, f32[]{:T(128)}) conditional(s32[]{:T(128)} %clamp.3, (s32[2,3,7]{2,1,0:T(4,128)S(1)}, s32[128,128]{1,0:T(8,128)S(1)}, f32[3,6,256,256]{3,2,1,0:T(8,128)}, f32[3,6,256,256]{3,2,1,0:T(8,128)}, s32[3,6]{1,0:T(4,128)}, /*index=5*/s32[3,6]{1,0:T(4,128)}) %tuple.103, ...), branch_computations={%region_3.4_spmd, %region_4.5_spmd, %region_5.6_spmd, %region_6.7_... | conditional | flops 4194313 | bytes 114692192 | solution.py:973
  25.5 0.6 reshape.245.own_ref
  26.1 0.1 copy.152
  26.1 0.5 slice_bitcast_fusion.10
  26.7 5.5 %pack.35 = (f32[9,256,256]{2,1,0:T(8,128)}, f32[9,256,256]{2,1,0:T(8,128)}, s32[74]{0:T(128)}) custom-call(s32[42]{0:T(128)} %reshape.245.own_ref, s32[128]{0:T(128)} %get-tuple-element.1005.left_ref, s32[128]{0:T(128)} %get-tuple-element.1004.right_ref, f32[18,256,256]{2,1,0:T(8,128)} %bitcast.255, f32[18,256,256]{2,1,0:T(8,128)} %bitcast.172), custom_call_target="tpu_custom_call" | custom-call | tf_op jit(solution)/shard_map/cond/branch_5_fun/pack/pallas_call | solution.py:300
  32.2 0.1 collective-permute-start.65
  32.3 0.0 copy-start.40
  32.3 5.3 %collective-permute-start.66 = (f32[9,256,256]{2,1,0:T(8,128)}, f32[9,256,256]{2,1,0:T(8,128)}, u32[]{:S(2)}, u32[]{:S(2)}) collective-permute-start(f32[9,256,256]{2,1,0:T(8,128)} %get-tuple-element.408), channel_id=1, source_target_pairs={{1,0},{2,1},{3,2},{4,3},{5,4},{6,5},{7,6},{8,7},{9,8},{10,9},{11,1... | collective-permute-start | bytes 7077896 | tf_op jit(solution)/shard_map/cond/branch_5_fun/ppermute | solution.py:943
  37.6 0.0 slice-done.20
  37.6 2.1 pack.34
  39.7 0.1 collective-permute-start.67
  39.8 5.3 %collective-permute-start.68 = (f32[2,256,256]{2,1,0:T(8,128)}, f32[2,256,256]{2,1,0:T(8,128)S(1)}, u32[]{:S(2)}, u32[]{:S(2)}) collective-permute-start(f32[2,256,256]{2,1,0:T(8,128)} %get-tuple-element.401), channel_id=1, source_target_pairs={{1,0},{2,1},{3,2},{4,3},{5,4},{6,5},{7,6},{8,7},{9,8},{10,9},{11,1... | collective-permute-start | bytes 1572872 | tf_op jit(solution)/shard_map/cond/branch_5_fun/ppermute | solution.py:943
  45.2 0.7 reshape.248.off_ref
  45.8 37.7 %own_rows.17 = (f32[21,256,256]{2,1,0:T(8,128)}, bf16[36,256,256]{2,1,0:T(8,128)(2,1)}, bf16[36,256,256]{2,1,0:T(8,128)(2,1)}, s32[4,3,384]{2,1,0:T(4,128)}, s32[36]{0:T(128)}) custom-call(s32[42]{0:T(128)} %reshape.245.own_ref, s32[128]{0:T(128)} %get-tuple-element.1005.left_ref, s32[128]{0:T(128)} %get-tuple-element.1004.right_ref, s32[18]{0:T(128)} %reshape.248.off_ref, ...), custom_call_target="tpu_custom_call" | custom-call | flops 1048576 | bytes 65536 | tf_op jit(solution)/shard_map/cond/branch_5_fun/own_rows/pallas_call | solution.py:485
  83.5 6.2 %collective-permute-done.65.low_ref = f32[9,256,256]{2,1,0:T(8,128)} collective-permute-done((f32[9,256,256]{2,1,0:T(8,128)}, f32[9,256,256]{2,1,0:T(8,128)}, u32[]{:S(2)}, u32[]{:S(2)}) %collective-permute-start.65) | collective-permute-done | bytes 2359328 | tf_op jit(solution)/shard_map/cond/branch_5_fun/ppermute | solution.py:943
  89.7 56.5 %collective-permute-done.66.high_ref = f32[9,256,256]{2,1,0:T(8,128)} collective-permute-done((f32[9,256,256]{2,1,0:T(8,128)}, f32[9,256,256]{2,1,0:T(8,128)}, u32[]{:S(2)}, u32[]{:S(2)}) %collective-permute-start.66) | collective-permute-done | bytes 2359328 | tf_op jit(solution)/shard_map/cond/branch_5_fun/ppermute | solution.py:943
  146.2 2.8 %help_rows.17 = (f32[6,256,256]{2,1,0:T(8,128)}, f32[6,256,256]{2,1,0:T(8,128)}, f32[1,1]{1,0:T(1,128)}) custom-call(s32[74]{0:T(128)} %get-tuple-element.406.sent_ref, s32[128]{0:T(128)} %get-tuple-element.1005.left_ref, s32[128]{0:T(128)} %get-tuple-element.1004.right_ref, s32[4,3,384]{2,1,0:T(4,128)} %get-tuple-element.404.lists_ref, ...), custom_call_target="tpu_custom_call" | custom-call | flops 1048576 | bytes 65536 | tf_op jit(solution)/shard_map/cond/branch_5_fun/help_rows/pallas_call | solution.py:626
  149.0 2.4 collective-permute-done.67.low_ref_2
  151.4 7.2 %collective-permute-done.68.high_ref_2 = f32[2,256,256]{2,1,0:T(8,128)S(1)} collective-permute-done((f32[2,256,256]{2,1,0:T(8,128)}, f32[2,256,256]{2,1,0:T(8,128)S(1)}, u32[]{:S(2)}, u32[]{:S(2)}) %collective-permute-start.68) | collective-permute-done | bytes 524320 | tf_op jit(solution)/shard_map/cond/branch_5_fun/ppermute | solution.py:943
  158.7 1.4 collective-permute-start.69
  160.1 3.9 %collective-permute-start.70 = (f32[6,256,256]{2,1,0:T(8,128)}, f32[6,256,256]{2,1,0:T(8,128)}, u32[]{:S(2)}, u32[]{:S(2)}) collective-permute-start(f32[6,256,256]{2,1,0:T(8,128)} %get-tuple-element.414), channel_id=1, source_target_pairs={{1,0},{2,1},{3,2},{4,3},{5,4},{6,5},{7,6},{8,7},{9,8},{10,9},{11,1... | collective-permute-start | bytes 4718600 | tf_op jit(solution)/shard_map/cond/branch_5_fun/ppermute | solution.py:943
  164.0 0.7 reshape.249.weight_ref
  164.7 23.3 %first_halo.17 = (f32[18,256,256]{2,1,0:T(8,128)S(1)}, f32[1,1]{1,0:T(1,128)}) custom-call(s32[4,3,384]{2,1,0:T(4,128)} %get-tuple-element.404.lists_ref, s32[128]{0:T(128)} %get-tuple-element.1005.left_ref, s32[128]{0:T(128)} %get-tuple-element.1004.right_ref, s32[18]{0:T(128)} %reshape.248.off_ref, s32[18]{0:T(128)} %reshape.249.weight_ref, ...), custom_call_target="tpu_custom_call" | custom-call | flops 1048576 | bytes 65536 | tf_op jit(solution)/shard_map/cond/branch_5_fun/first_halo/pallas_call | solution.py:716
  189.4 38.6 %collective-permute-start.73 = (f32[1,1]{1,0:T(1,128)}, f32[1,1]{1,0:T(1,128)}, u32[]{:S(2)}, u32[]{:S(2)}) collective-permute-start(f32[1,1]{1,0:T(1,128)} %add.273), channel_id=1, source_target_pairs={{0,3},{1,2},{2,1},{3,0},{4,7},{5,6},{6,5},{7,4},{8,11},{9,10},{10,... | collective-permute-start | bytes 20 | tf_op jit(solution)/shard_map/cond/branch_5_fun/ppermute | solution.py:879
  228.0 3.2 %collective-permute-start.72 = (f32[1,1]{1,0:T(1,128)}, f32[1,1]{1,0:T(1,128)}, u32[]{:S(2)}, u32[]{:S(2)}) collective-permute-start(f32[1,1]{1,0:T(1,128)} %add.273), channel_id=1, source_target_pairs={{0,2},{1,3},{2,0},{3,1},{4,6},{5,7},{6,4},{7,5},{8,10},{9,11},{10,... | collective-permute-start | bytes 20 | tf_op jit(solution)/shard_map/cond/branch_5_fun/ppermute | solution.py:879
  231.1 1.3 collective-permute-start.71
  232.4 2.2 collective-permute-done.71
  236.5 1.4 collective-permute-start.76
  237.8 1.3 collective-permute-start.75
  239.1 1.5 collective-permute-start.74
  241.3 0.2 collective-permute-done.75
  242.7 2.1 collective-permute-start.77
  244.7 1.6 collective-permute-done.77
  246.9 0.0 collective-permute-done.69.low_ref
  246.9 0.0 collective-permute-done.70.high_ref
  246.9 4.6 %last_halo.17 = f32[18,256,256]{2,1,0:T(8,128)S(1)} custom-call(s32[4,3,384]{2,1,0:T(4,128)} %get-tuple-element.404.lists_ref, s32[36]{0:T(128)} %get-tuple-element.405.used_ref, s32[128]{0:T(128)} %get-tuple-element.1005.left_ref, s32[128]{0:T(128)} %get-tuple-element.1004.right_ref, s32[18]{0:T(128)} %reshape.248.off_ref, ...), custom_call_target="tpu_custom_call", output_to_operand_aliasing={{}: (9, {})} | custom-call | flops 1048576 | bytes 65536 | tf_op jit(solution)/shard_map/cond/branch_5_fun/last_halo/pallas_call | solution.py:852
  251.6 0.0 copy-start.5
  251.6 2.2 copy-done.5
  (44 shorter events, 0.2 us)
Async XLA Ops:
  1.4 7.2 %collective-permute-start.158 = (s32[1,3,18]{2,1,0:T(4,128)S(1)}, s32[1,3,18]{2,1,0:T(4,128)S(1)}, u32[]{:S(2)}, u32[]{:S(2)}) collective-permute-start(s32[1,3,18]{2,1,0:T(4,128)S(1)} %get-tuple-element.993), channel_id=1, source_target_pairs={{0,3},{1,2},{2,1},{3,0},{4,7},{5,6},{6,5},{7,4},{8,11},{9,10},{10,... | collective-permute-start | bytes 656 | tf_op jit(solution)/shard_map/ppermute | solution.py:879
  6.5 4.5 %collective-permute-start.157 = (s32[1,3,18]{2,1,0:T(4,128)S(1)}, s32[1,3,18]{2,1,0:T(4,128)S(1)}, u32[]{:S(2)}, u32[]{:S(2)}) collective-permute-start(s32[1,3,18]{2,1,0:T(4,128)S(1)} %get-tuple-element.993), channel_id=1, source_target_pairs={{0,2},{1,3},{2,0},{3,1},{4,6},{5,7},{6,4},{7,5},{8,10},{9,11},{10,... | collective-permute-start | bytes 656 | tf_op jit(solution)/shard_map/ppermute | solution.py:879
  6.5 4.5 %collective-permute-start.156 = (s32[1,3,18]{2,1,0:T(4,128)S(1)}, s32[1,3,18]{2,1,0:T(4,128)S(1)}, u32[]{:S(2)}, u32[]{:S(2)}) collective-permute-start(s32[1,3,18]{2,1,0:T(4,128)S(1)} %get-tuple-element.993), channel_id=1, source_target_pairs={{0,1},{1,0},{2,3},{3,2},{4,5},{5,4},{6,7},{7,6},{8,9},{9,8},{10,11... | collective-permute-start | bytes 656 | tf_op jit(solution)/shard_map/ppermute | solution.py:879
  11.0 3.8 %collective-permute-start.161 = (s32[4,3,18]{2,1,0:T(4,128)S(1)}, s32[4,3,18]{2,1,0:T(4,128)S(1)}, u32[]{:S(2)}, u32[]{:S(2)}) collective-permute-start(s32[4,3,18]{2,1,0:T(4,128)S(1)} %pad_add_fusion.2), channel_id=1, source_target_pairs={{0,12},{1,13},{2,14},{3,15},{4,8},{5,9},{6,10},{7,11},{8,4},{9,5},... | collective-permute-start | bytes 2600 | tf_op jit(solution)/shard_map/ppermute | solution.py:879
  11.0 3.7 %collective-permute-start.160 = (s32[4,3,18]{2,1,0:T(4,128)S(1)}, s32[4,3,18]{2,1,0:T(4,128)S(1)}, u32[]{:S(2)}, u32[]{:S(2)}) collective-permute-start(s32[4,3,18]{2,1,0:T(4,128)S(1)} %pad_add_fusion.2), channel_id=1, source_target_pairs={{0,8},{1,9},{2,10},{3,11},{4,12},{5,13},{6,14},{7,15},{8,0},{9,1},... | collective-permute-start | bytes 2600 | tf_op jit(solution)/shard_map/ppermute | solution.py:879
  12.6 1.2 collective-permute-start.159
  14.8 4.0 %collective-permute-start.162 = (s32[16,3,18]{2,1,0:T(4,128)S(1)}, s32[16,3,18]{2,1,0:T(4,128)S(1)}, u32[]{:S(2)}, u32[]{:S(2)}) collective-permute-start(s32[16,3,18]{2,1,0:T(4,128)S(1)} %get-tuple-element.1018), channel_id=1, source_target_pairs={{0,16},{1,17},{2,18},{3,19},{4,20},{5,21},{6,22},{7,23},{8,24},{9,... | collective-permute-start | bytes 10376 | tf_op jit(solution)/shard_map/ppermute | solution.py:879
  26.7 10.9 %slice-start.20 = ((s8[4718592]{0:T(1024)(128)(4,1)}), s8[4194304]{0:T(1024)(128)(4,1)S(1)}, s32[]{:S(2)}) async-start(s8[4718592]{0:T(1024)(128)(4,1)} %bitcast.175), calls=%async_computation.20 | async-start | bytes 8388608 | tf_op jit(solution)/shard_map/cond
  26.7 10.9 %slice-start.21 = ((s8[4718592]{0:T(1024)(128)(4,1)}), s8[524288]{0:T(1024)(128)(4,1)S(1)}, s32[]{:S(2)}) async-start(s8[4718592]{0:T(1024)(128)(4,1)} %bitcast.175), calls=%async_computation.21 | async-start | bytes 1048576 | tf_op jit(solution)/shard_map/cond
  32.2 57.5 %collective-permute-start.65 = (f32[9,256,256]{2,1,0:T(8,128)}, f32[9,256,256]{2,1,0:T(8,128)}, u32[]{:S(2)}, u32[]{:S(2)}) collective-permute-start(f32[9,256,256]{2,1,0:T(8,128)} %get-tuple-element.407), channel_id=1, source_target_pairs={{0,1},{1,2},{2,3},{3,4},{4,5},{5,6},{6,7},{7,8},{8,9},{9,10},{10,1... | collective-permute-start | bytes 7077896 | tf_op jit(solution)/shard_map/cond/branch_5_fun/ppermute | solution.py:943
  32.3 12.9 %copy-start.40 = (s32[3,6]{1,0:T(4,128)S(1)}, s32[3,6]{1,0:T(4,128)}, u32[]{:S(2)}) copy-start(s32[3,6]{1,0:T(4,128)} %get-tuple-element.403) | copy-start | bytes 220 | tf_op jit(solution)/shard_map/cond
  32.3 113.9 %collective-permute-start.66 = (f32[9,256,256]{2,1,0:T(8,128)}, f32[9,256,256]{2,1,0:T(8,128)}, u32[]{:S(2)}, u32[]{:S(2)}) collective-permute-start(f32[9,256,256]{2,1,0:T(8,128)} %get-tuple-element.408), channel_id=1, source_target_pairs={{1,0},{2,1},{3,2},{4,3},{5,4},{6,5},{7,6},{8,7},{9,8},{10,9},{11,1... | collective-permute-start | bytes 7077896 | tf_op jit(solution)/shard_map/cond/branch_5_fun/ppermute | solution.py:943
  39.7 111.7 %collective-permute-start.67 = (f32[2,256,256]{2,1,0:T(8,128)}, f32[2,256,256]{2,1,0:T(8,128)S(1)}, u32[]{:S(2)}, u32[]{:S(2)}) collective-permute-start(f32[2,256,256]{2,1,0:T(8,128)} %get-tuple-element.400), channel_id=1, source_target_pairs={{0,1},{1,2},{2,3},{3,4},{4,5},{5,6},{6,7},{7,8},{8,9},{9,10},{10,1... | collective-permute-start | bytes 1572872 | tf_op jit(solution)/shard_map/cond/branch_5_fun/ppermute | solution.py:943
  39.8 118.8 %collective-permute-start.68 = (f32[2,256,256]{2,1,0:T(8,128)}, f32[2,256,256]{2,1,0:T(8,128)S(1)}, u32[]{:S(2)}, u32[]{:S(2)}) collective-permute-start(f32[2,256,256]{2,1,0:T(8,128)} %get-tuple-element.401), channel_id=1, source_target_pairs={{1,0},{2,1},{3,2},{4,3},{5,4},{6,5},{7,6},{8,7},{9,8},{10,9},{11,1... | collective-permute-start | bytes 1572872 | tf_op jit(solution)/shard_map/cond/branch_5_fun/ppermute | solution.py:943
  45.2 101.0 %slice-start.22 = ((s8[4718592]{0:T(1024)(128)(4,1)}), s8[524288]{0:T(1024)(128)(4,1)S(1)}, s32[]{:S(2)}) async-start(s8[4718592]{0:T(1024)(128)(4,1)} %bitcast.178), calls=%async_computation.22 | async-start | bytes 1048576 | tf_op jit(solution)/shard_map/cond
  45.8 100.4 %slice-start.23 = ((s8[4718592]{0:T(1024)(128)(4,1)}), s8[4194304]{0:T(1024)(128)(4,1)S(1)}, s32[]{:S(2)}) async-start(s8[4718592]{0:T(1024)(128)(4,1)} %bitcast.178), calls=%async_computation.23 | async-start | bytes 8388608 | tf_op jit(solution)/shard_map/cond
  146.2 17.8 %copy-start.52 = (s32[3,6]{1,0:T(4,128)S(1)}, s32[3,6]{1,0:T(4,128)}, u32[]{:S(2)}) copy-start(s32[3,6]{1,0:T(4,128)} %get-tuple-element.415) | copy-start | bytes 220 | tf_op jit(solution)/shard_map/cond
  151.4 13.2 %copy-start.24 = (f32[2,256,256]{2,1,0:T(8,128)}, f32[2,256,256]{2,1,0:T(8,128)S(1)}, u32[]{:S(2)}) copy-start(f32[2,256,256]{2,1,0:T(8,128)S(1)} %collective-permute-done.67.low_ref_2) | copy-start | bytes 1572868 | tf_op jit(solution)/shard_map/cond
  158.7 6.0 %copy-start.29 = (f32[2,256,256]{2,1,0:T(8,128)}, f32[2,256,256]{2,1,0:T(8,128)S(1)}, u32[]{:S(2)}) copy-start(f32[2,256,256]{2,1,0:T(8,128)S(1)} %collective-permute-done.68.high_ref_2) | copy-start | bytes 1572868 | tf_op jit(solution)/shard_map/cond
  158.7 88.3 %collective-permute-start.69 = (f32[6,256,256]{2,1,0:T(8,128)}, f32[6,256,256]{2,1,0:T(8,128)}, u32[]{:S(2)}, u32[]{:S(2)}) collective-permute-start(f32[6,256,256]{2,1,0:T(8,128)} %get-tuple-element.413), channel_id=1, source_target_pairs={{0,1},{1,2},{2,3},{3,4},{4,5},{5,6},{6,7},{7,8},{8,9},{9,10},{10,1... | collective-permute-start | bytes 4718600 | tf_op jit(solution)/shard_map/cond/branch_5_fun/ppermute | solution.py:943
  160.1 86.8 %collective-permute-start.70 = (f32[6,256,256]{2,1,0:T(8,128)}, f32[6,256,256]{2,1,0:T(8,128)}, u32[]{:S(2)}, u32[]{:S(2)}) collective-permute-start(f32[6,256,256]{2,1,0:T(8,128)} %get-tuple-element.414), channel_id=1, source_target_pairs={{1,0},{2,1},{3,2},{4,3},{5,4},{6,5},{7,6},{8,7},{9,8},{10,9},{11,1... | collective-permute-start | bytes 4718600 | tf_op jit(solution)/shard_map/cond/branch_5_fun/ppermute | solution.py:943
  189.4 45.9 %collective-permute-start.73 = (f32[1,1]{1,0:T(1,128)}, f32[1,1]{1,0:T(1,128)}, u32[]{:S(2)}, u32[]{:S(2)}) collective-permute-start(f32[1,1]{1,0:T(1,128)} %add.273), channel_id=1, source_target_pairs={{0,3},{1,2},{2,1},{3,0},{4,7},{5,6},{6,5},{7,4},{8,11},{9,10},{10,... | collective-permute-start | bytes 20 | tf_op jit(solution)/shard_map/cond/branch_5_fun/ppermute | solution.py:879
  228.0 7.3 %collective-permute-start.72 = (f32[1,1]{1,0:T(1,128)}, f32[1,1]{1,0:T(1,128)}, u32[]{:S(2)}, u32[]{:S(2)}) collective-permute-start(f32[1,1]{1,0:T(1,128)} %add.273), channel_id=1, source_target_pairs={{0,2},{1,3},{2,0},{3,1},{4,6},{5,7},{6,4},{7,5},{8,10},{9,11},{10,... | collective-permute-start | bytes 20 | tf_op jit(solution)/shard_map/cond/branch_5_fun/ppermute | solution.py:879
  231.1 3.5 %collective-permute-start.71 = (f32[1,1]{1,0:T(1,128)}, f32[1,1]{1,0:T(1,128)}, u32[]{:S(2)}, u32[]{:S(2)}) collective-permute-start(f32[1,1]{1,0:T(1,128)} %add.273), channel_id=1, source_target_pairs={{0,1},{1,0},{2,3},{3,2},{4,5},{5,4},{6,7},{7,6},{8,9},{9,8},{10,11... | collective-permute-start | bytes 20 | tf_op jit(solution)/shard_map/cond/branch_5_fun/ppermute | solution.py:879
  236.5 4.8 %collective-permute-start.76 = (f32[1,1]{1,0:T(1,128)}, f32[1,1]{1,0:T(1,128)}, u32[]{:S(2)}, u32[]{:S(2)}) collective-permute-start(f32[1,1]{1,0:T(1,128)} %add.276), channel_id=1, source_target_pairs={{0,12},{1,13},{2,14},{3,15},{4,8},{5,9},{6,10},{7,11},{8,4},{9,5},... | collective-permute-start | bytes 20 | tf_op jit(solution)/shard_map/cond/branch_5_fun/ppermute | solution.py:879
  237.8 3.6 %collective-permute-start.75 = (f32[1,1]{1,0:T(1,128)}, f32[1,1]{1,0:T(1,128)}, u32[]{:S(2)}, u32[]{:S(2)}) collective-permute-start(f32[1,1]{1,0:T(1,128)} %add.276), channel_id=1, source_target_pairs={{0,8},{1,9},{2,10},{3,11},{4,12},{5,13},{6,14},{7,15},{8,0},{9,1},... | collective-permute-start | bytes 20 | tf_op jit(solution)/shard_map/cond/branch_5_fun/ppermute | solution.py:879
  239.1 1.5 collective-permute-start.74
  242.7 3.7 %collective-permute-start.77 = (f32[1,1]{1,0:T(1,128)}, f32[1,1]{1,0:T(1,128)}, u32[]{:S(2)}, u32[]{:S(2)}) collective-permute-start(f32[1,1]{1,0:T(1,128)} %add.279), channel_id=1, source_target_pairs={{0,16},{1,17},{2,18},{3,19},{4,20},{5,21},{6,22},{7,23},{8,24},{9,... | collective-permute-start | bytes 20 | tf_op jit(solution)/shard_map/cond/branch_5_fun/ppermute | solution.py:879
  251.6 2.2 copy-start.5
